TPU v7x, 32 devices: a whole 2x2x4 slice. The times are simulated.
32 devices in a mesh: dp: 8 (over z, core), seq: 4 (over y, x).
Axes of the slice: x: 2, y: 2, z: 4, core: 2. Of those that a mesh axis runs over, the one named last changes fastest.
Arguments:
- tokens: bfloat16 [8, 2048, 1024], P('dp', 'seq'), may hold values from -6 to 6
- input_weight: bfloat16 [1024, 3072], P(('dp', 'seq')), may hold values from -0.1875 to 0.1875
- input_bias: bfloat16 [3072], P(('dp', 'seq')), may hold values from -1.75 to 1.75
- output_weight: bfloat16 [1024, 1024], P(('dp', 'seq')), may hold values from -4 to 4
- output_bias: bfloat16 [1024], P(('dp', 'seq')), may hold values from -1.75 to 1.75
- up_weight: bfloat16 [1024, 4096], P(('dp', 'seq')), may hold values from -0.1875 to 0.1875
- up_bias: bfloat16 [4096], P(('dp', 'seq')), may hold values from -1.75 to 1.75
- down_weight: bfloat16 [4096, 1024], P(('dp', 'seq')), may hold values from -0.09375 to 0.09375
- down_bias: bfloat16 [1024], P(('dp', 'seq')), may hold values from -1.75 to 1.75
- attention_gain: bfloat16 [1024], P(('dp', 'seq')), may hold values from 0.099609375 to 1.8984375
- attention_shift: bfloat16 [1024], P(('dp', 'seq')), may hold values from -1.75 to 1.75
- feedforward_gain: bfloat16 [1024], P(('dp', 'seq')), may hold values from 0.099609375 to 1.8984375
- feedforward_shift: bfloat16 [1024], P(('dp', 'seq')), may hold values from -1.75 to 1.75
- cotangent: bfloat16 [8, 2048, 1024], P('dp', 'seq'), may hold values from -6 to 6
Outputs:
- output: bfloat16 [8, 2048, 1024], P('dp', 'seq')
- token_grad: bfloat16 [8, 2048, 1024], P('dp', 'seq')
- input_weight_grad: float32 [1024, 3072], P(('dp', 'seq'))
- input_bias_grad: float32 [2048], P(('dp', 'seq'))
- value_bias_grad: float32 [1024], P(('dp', 'seq'))
- output_weight_grad: float32 [1024, 1024], P(('dp', 'seq'))
- output_bias_grad: float32 [1024], P(('dp', 'seq'))
- up_weight_grad: float32 [1024, 4096], P(('dp', 'seq'))
- up_bias_grad: float32 [4096], P(('dp', 'seq'))
- down_weight_grad: float32 [4096, 1024], P(('dp', 'seq'))
- down_bias_grad: float32 [1024], P(('dp', 'seq'))
- attention_gain_grad: float32 [1024], P(('dp', 'seq'))
- attention_shift_grad: float32 [1024], P(('dp', 'seq'))
- feedforward_gain_grad: float32 [1024], P(('dp', 'seq'))
- feedforward_shift_grad: float32 [1024], P(('dp', 'seq'))
All inputs are finite; a program needn't handle non-finite values.
Results may differ from a plain program's by a relative error of at most 0.014.
Values may be sent and summed in bfloat16 or wider, within the bound.
No kernel may reach another device: no remote copies, remote signals or barrier semaphores. Data moves between devices by JAX's collectives and lax.ppermute only.
A program may use at most 256 MiB of HBM per device.

v0:
```python
import functools
import math

import jax
import jax.numpy as jnp
import numpy as np
from jax import lax
from jax.experimental import pallas as pl
from jax.experimental.pallas import tpu as pltpu
from jax.sharding import PartitionSpec as P

HEADS = 16
ROT = 16

norm_eps = 1e-05
masked_score = -1e30
low = jnp.bfloat16
full = jnp.float32
kernel_memory = 56 * 1024 * 1024


def place_at(pieces, spots, axis):
    count = len(pieces)
    shape = list(pieces[0].shape)
    shape.insert(axis, count)
    held = jnp.zeros(shape, pieces[0].dtype)
    for piece, spot in zip(pieces, spots):
        held = lax.dynamic_update_index_in_dim(held, piece, spot, axis)
    return held


def pick(array, spot, axis):
    return lax.dynamic_index_in_dim(array, spot, axis, keepdims=False)


def effort(micros):
    return pl.CostEstimate(flops=int(micros * 1.1e9), bytes_accessed=1, transcendentals=0)


anywhere = pl.BlockSpec(memory_space=pl.ANY)


def pass_kernel(*refs):
    del refs


def after_big(array, *others):
    return pl.pallas_call(
        pass_kernel,
        in_specs=[anywhere] * (1 + len(others)),
        out_specs=anywhere,
        out_shape=jax.ShapeDtypeStruct(array.shape, array.dtype),
        input_output_aliases={0: 0},
        name="after_big",
    )(array, *others)


def join_kernel(first, second, *refs):
    rows = first.shape[0]
    refs[-1][:rows, :] = first[...]
    refs[-1][rows:, :] = second[...]


def join(first, second, wait):
    vmem = pl.BlockSpec(memory_space=pltpu.VMEM)
    return pl.pallas_call(
        join_kernel,
        in_specs=[vmem, vmem] + [anywhere] * len(wait),
        out_specs=vmem,
        out_shape=jax.ShapeDtypeStruct((first.shape[0] + second.shape[0], first.shape[1]), first.dtype),
        compiler_params=pltpu.CompilerParams(vmem_limit_bytes=kernel_memory),
        name="join",
    )(first, second, *wait)


def after_kernel(source, *refs):
    refs[-1][...] = source[...]


def after(array, *others):
    vmem = pl.BlockSpec(memory_space=pltpu.VMEM)
    return pl.pallas_call(
        after_kernel,
        in_specs=[vmem] + [anywhere] * len(others),
        out_specs=vmem,
        out_shape=jax.ShapeDtypeStruct(array.shape, array.dtype),
        compiler_params=pltpu.CompilerParams(vmem_limit_bytes=kernel_memory),
        name="after",
    )(array, *others)


def chosen_units(ref, rank, ranks, units):
    runs = ref.shape[1] // (ranks * units)
    parts = []
    for run in range(runs):
        first = run * ranks * units
        if units % 128 == 0:
            parts.append(ref[:, pl.ds(pl.multiple_of(first + rank * units, 128), units)])
        else:
            whole = ref[:, first : first + ranks * units]
            part = jnp.zeros((ref.shape[0], units), ref.dtype)
            for r in range(ranks):
                part = jnp.where(rank == r, whole[:, r * units : (r + 1) * units], part)
            parts.append(part)
    return jnp.concatenate(parts, 1)


def deal_kernel(ranks, groups, vectors, units, place, in_ref, up_ref, *refs):
    shard, columns = in_ref.shape
    width = columns // 3
    span = width // ranks
    lanes = span // groups
    for k in range(ranks):
        rank = place[0] ^ k
        dealt = refs[vectors + k]
        dealt[:shard, 3 * span :] = jnp.zeros((shard, span), low)

        def part(start):
            first = start + rank * span
            if span % 128 == 0:
                return in_ref[:, pl.ds(pl.multiple_of(first, 128), span)]
            whole = in_ref[:, start : start + width]
            chosen = jnp.zeros((shard, span), low)
            for r in range(ranks):
                chosen = jnp.where(rank == r, whole[:, r * span : (r + 1) * span], chosen)
            return chosen

        for kind in range(3):
            mine = part(kind * width)
            for group in range(groups):
                target = (group * 3 + kind) * lanes
                dealt[:shard, target : target + lanes] = mine[:, group * lanes : (group + 1) * lanes]
        dealt[shard + 16 :, :] = chosen_units(up_ref, rank, ranks, units)
        dealt[shard : shard + 16, :] = jnp.zeros((16, 4 * span), low)
        for i, ref in enumerate(refs[:vectors]):
            dealt[shard + i : shard + i + 1, : ref.shape[1]] = ref[...]


def deal(place, input_weight, up_weight, vectors, ranks, groups, units):
    shard, columns = input_weight.shape
    arrays = [input_weight, up_weight] + [v[None] for v in vectors]
    shape = (2 * shard + 16, 4 * columns // (3 * ranks))
    vmem = pl.BlockSpec(memory_space=pltpu.VMEM)
    return pl.pallas_call(
        functools.partial(deal_kernel, ranks, groups, len(vectors), units),
        in_specs=[pl.BlockSpec(memory_space=pltpu.SMEM)] + [vmem] * len(arrays),
        out_specs=[vmem] * ranks,
        out_shape=[jax.ShapeDtypeStruct(shape, low)] * ranks,
        compiler_params=pltpu.CompilerParams(vmem_limit_bytes=kernel_memory),
        name="deal",
    )(place, *arrays)


def gather_heads_kernel(count, shard, place, *refs):
    out, units = refs[count:]
    columns = out.shape[1]
    for k in range(count):
        rank = place[0] ^ k
        if shard % 16 == 0:
            here = pl.ds(pl.multiple_of(rank * shard, 16), shard)
            out[here, :] = refs[k][:shard, :columns]
            units[here, :] = refs[k][shard + 16 :, :]
        else:
            for r in range(count):

                @pl.when(rank == r)
                def _(r=r, k=k):
                    out[r * shard : (r + 1) * shard, :] = refs[k][:shard, :columns]
                    units[r * shard : (r + 1) * shard, :] = refs[k][shard + 16 :, :]

    vectors = []
    for r in range(count):
        mine = jnp.zeros((8, columns), full)
        for k in range(count):
            rows = refs[k][shard : shard + 16, :columns].astype(full)[:8]
            mine = jnp.where((place[0] ^ k) == r, rows, mine)
        vectors.append(mine)
    out[count * shard :, :] = jnp.concatenate(vectors, 0).astype(low)


def gather_heads(place, pieces, shard):
    count = len(pieces)
    wide = pieces[0].shape[1]
    vmem = pl.BlockSpec(memory_space=pltpu.VMEM)
    return pl.pallas_call(
        functools.partial(gather_heads_kernel, count, shard),
        in_specs=[pl.BlockSpec(memory_space=pltpu.SMEM)] + [vmem] * count,
        out_specs=[vmem, vmem],
        out_shape=[
            jax.ShapeDtypeStruct((count * shard + count * 8, wide // 4 * 3), low),
            jax.ShapeDtypeStruct((count * shard, wide), low),
        ],
        compiler_params=pltpu.CompilerParams(vmem_limit_bytes=kernel_memory),
        name="gather_heads",
    )(place, *pieces)


def cut_kernel(x_ref, y_ref, *refs):
    first, second = refs[-2:]
    first[...] = x_ref[...]
    second[...] = y_ref[...]


def cut(x, y, wait):
    seqs, block, width = x.shape
    half = (seqs, block // 2, width)
    return pl.pallas_call(
        cut_kernel,
        grid=(1,),
        in_specs=[pl.BlockSpec(half, lambda i: (0, 0, 0)), pl.BlockSpec(half, lambda i: (0, 1, 0))]
        + [anywhere] * len(wait),
        out_specs=[pl.BlockSpec(half, lambda i: (0, 0, 0))] * 2,
        out_shape=[jax.ShapeDtypeStruct(half, x.dtype)] * 2,
        compiler_params=pltpu.CompilerParams(vmem_limit_bytes=kernel_memory),
        name="cut",
    )(x, y, *wait)


def lay_columns_kernel(count, place, *refs):
    out = refs[count]
    span = refs[0].shape[1]
    for k in range(count):
        rank = place[0] ^ k
        if span % 128 == 0:
            out[:, pl.ds(pl.multiple_of(rank * span, 128), span)] = refs[k][...]
        else:
            for r in range(count):

                @pl.when(rank == r)
                def _(r=r, k=k):
                    out[:, r * span : (r + 1) * span] = refs[k][...]


def lay_columns(place, pieces):
    count = len(pieces)
    rows, span = pieces[0].shape
    vmem = pl.BlockSpec(memory_space=pltpu.VMEM)
    return pl.pallas_call(
        functools.partial(lay_columns_kernel, count),
        in_specs=[pl.BlockSpec(memory_space=pltpu.SMEM)] + [vmem] * count,
        out_specs=vmem,
        out_shape=jax.ShapeDtypeStruct((rows, count * span), pieces[0].dtype),
        compiler_params=pltpu.CompilerParams(vmem_limit_bytes=kernel_memory),
        name="lay_columns",
    )(place, *pieces)


def lay_kernel(count, place, *refs):
    out = refs[count]
    for k in range(count):
        out[place[0] ^ k] = refs[k][...]


def lay(place, pieces):
    count = len(pieces)
    shape = (count,) + pieces[0].shape
    return pl.pallas_call(
        functools.partial(lay_kernel, count),
        grid_spec=pltpu.PrefetchScalarGridSpec(
            num_scalar_prefetch=1,
            grid=(1,),
            in_specs=[pl.BlockSpec(p.shape, lambda i, place, n=p.ndim: (0,) * n) for p in pieces],
            out_specs=pl.BlockSpec(shape, lambda i, place: (0,) * len(shape)),
        ),
        out_shape=jax.ShapeDtypeStruct(shape, pieces[0].dtype),
        compiler_params=pltpu.CompilerParams(vmem_limit_bytes=kernel_memory),
        name="lay",
    )(place, *pieces)


class Layout:
    def __init__(self):
        self.dp = lax.axis_size("dp")
        self.seq = lax.axis_size("seq")
        self.rank = lax.axis_index("seq")

    def seq_swap(self, array, k):
        return lax.ppermute(array, "seq", [(i, i ^ k) for i in range(self.seq)])

    def to_heads(self, array):
        pairs = [(f, (f % self.dp) * self.seq + f // self.dp) for f in range(self.dp * self.seq)]
        return lax.ppermute(array, ("dp", "seq"), pairs)

    def from_heads(self, array):
        pairs = [((f % self.dp) * self.seq + f // self.dp, f) for f in range(self.dp * self.seq)]
        return lax.ppermute(array, ("dp", "seq"), pairs)

    def seq_exchange(self, piece_for):
        return [piece_for(self.rank)] + [
            self.seq_swap(piece_for(self.rank ^ k), k) for k in range(1, self.seq)
        ]

    def seq_trade(self, array, place):
        return lay(place, self.seq_exchange(lambda spot: pick(array, spot, 0)))

    def seq_spots(self):
        return [self.rank ^ k for k in range(self.seq)]

    def seq_gather_direct(self, array):
        return [array] + [self.seq_swap(array, k) for k in range(1, self.seq)]

    def seq_gather(self, array):
        if self.seq != 4:
            return self.seq_gather_direct(array)
        return self.seq_gather_far(self.seq_gather_near(array))

    def seq_gather_near(self, array):
        if self.seq != 4:
            return self.seq_gather_direct(array)
        return [array, self.seq_swap(array, 1), self.seq_swap(array, 2)]

    def seq_gather_far(self, near, *wait):
        if self.seq != 4:
            return near
        first, second = cut(near[1], near[2], wait)
        return near + [self.seq_swap(first, 2), self.seq_swap(second, 1)]

    def seq_reduce_far(self, part):
        half = part.shape[1] // 2
        return self.seq_swap(part[:, half:], 2), self.seq_swap(part[:, :half], 1)

    def seq_reduce_near(self, parts, far):
        half = parts[0].shape[1] // 2
        for_x, for_y = (a.astype(full) for a in far)
        p1, p2 = parts
        p1 = jnp.concatenate([p1[:, :half], (p1[:, half:].astype(full) + for_x).astype(low)], 1)
        p2 = jnp.concatenate([(p2[:, :half].astype(full) + for_y).astype(low), p2[:, half:]], 1)
        return self.seq_swap(p1, 1), self.seq_swap(p2, 2)

    def seq_turnover(self, array):
        return lax.all_to_all(array, "seq", 0, 0, tiled=True)

    def z_turn(self, array, k):
        return lax.ppermute(array, "dp", [(i, (i + k) % self.dp) for i in range(self.dp)])

    def small_reduce(self, array):
        array = sum(self.seq_exchange(lambda spot: pick(array, spot, 1)))
        cores = 2 if self.dp % 2 == 0 else 1
        here = lax.axis_index("dp")
        core, z = here % cores, here // cores
        line = self.dp // cores
        pairs = array.reshape((line, cores) + array.shape[1:])
        if cores == 2:
            swap = [(i, i ^ 1) for i in range(self.dp)]
            array = pick(pairs, core, 1) + lax.ppermute(pick(pairs, 1 - core, 1), "dp", swap)
        else:
            array = pairs[:, 0]
        total = pick(array, z, 0)
        for k in range(1, line):
            total = total + self.z_turn(pick(array, (z + k) % line, 0), k * cores)
        return total

    def dp_gather(self, array):
        return lax.all_gather(array, "dp", axis=0, tiled=False)

    def dp_reduce(self, array):
        return lax.psum_scatter(array, "dp", scatter_dimension=0, tiled=False)


def rotary_tables(length, lanes, head_dim):
    half = ROT // 2
    exponent = -np.arange(0, ROT, 2, dtype=np.float32) / np.float32(ROT)
    frequency = np.float32(10000.0) ** exponent
    phase = np.arange(length, dtype=np.float32)[:, None] * frequency[None, :]
    cosine = np.ones((length, head_dim), np.float32)
    sine = np.zeros((length, head_dim), np.float32)
    cosine[:, :half] = cosine[:, half:ROT] = np.cos(phase)
    sine[:, :half] = -np.sin(phase)
    sine[:, half:ROT] = np.sin(phase)
    copies = lanes // head_dim
    return np.tile(cosine, (1, copies)), np.tile(sine, (1, copies))


def roll_lanes(x, shift):
    size = x.shape[-1]
    if size % 128 == 0:
        return pltpu.roll(x, shift % size, x.ndim - 1)
    return jnp.roll(x, shift, -1)


def turn(x, cosine, sine, head_dim):
    half = ROT // 2
    lane = lax.broadcasted_iota(jnp.int32, x.shape, 1) % head_dim
    swapped = jnp.where(lane < half, roll_lanes(x, -half), roll_lanes(x, half))
    return x * cosine + swapped * sine


def normalised(x):
    mean = jnp.mean(x, axis=-1, keepdims=True)
    centered = x - mean
    variance = jnp.mean(centered * centered, axis=-1, keepdims=True)
    rstd = lax.rsqrt(variance + norm_eps)
    return centered * rstd, rstd


def project_kernel(head_dim, lanes, shard, columns, stacked, count, place, head_ref, bias_ref, norms_ref, cos_ref, sin_ref, *refs):
    pieces, (x_out, attn_ref, ff_ref, qkv_ref, weight_ref) = refs[:count], refs[-5:]
    block, width = x_out.shape
    step = pl.program_id(0)

    @pl.when(step == 0)
    def _():
        weight_ref[...] = head_ref[:, :shard, :columns].reshape(width, columns)

    if stacked:
        x_out[...] = pieces[0][...]
    else:
        first = 0
        for piece in pieces:
            rows = piece.shape[0]
            inside = first % block

            @pl.when(step == first // block)
            def _(piece=piece, inside=inside, rows=rows):
                x_out[inside : inside + rows, :] = piece[...]

            first += rows
    unit, _ = normalised(x_out[...].astype(full))
    normed = (unit * norms_ref[0:1, :] + norms_ref[1:2, :]).astype(low)
    attn_ref[...] = normed
    ff_ref[...] = (unit * norms_ref[2:3, :] + norms_ref[3:4, :]).astype(low)
    mixed = jnp.dot(normed, weight_ref[...], preferred_element_type=full) + bias_ref[...]
    cosine, sine = cos_ref[...], sin_ref[...]
    for group in range(columns // lanes):
        span = slice(group * lanes, (group + 1) * lanes)
        part = mixed[:, span]
        if group % 3 < 2:
            part = turn(part, cosine, sine, head_dim)
        qkv_ref[:, span] = part.astype(low)


def project(place, pieces, head, bias, norms, cosine, sine, block, seqs, lanes, head_dim, shard, rows, start=0, earlier=()):
    stacked = len(pieces) == 1
    width = pieces[0].shape[1]
    columns = bias.shape[1]
    whole = lambda i, place: (0, 0)
    step = lambda i, place: (i + start, 0)
    spot = lambda i, place: (((i + start) // seqs) ^ place[0], 0)
    if stacked:
        piece_specs = [pl.BlockSpec((block, width), step)]
    else:
        piece_specs = [pl.BlockSpec(p.shape, whole) for p in pieces]
    return pl.pallas_call(
        functools.partial(project_kernel, head_dim, lanes, shard, columns, stacked, len(pieces)),
        grid_spec=pltpu.PrefetchScalarGridSpec(
            num_scalar_prefetch=1,
            grid=(sum(p.shape[0] for p in pieces) // block,),
            in_specs=[
                pl.BlockSpec(head.shape, lambda i, place: (0, 0, 0)),
                pl.BlockSpec((1, columns), whole),
                pl.BlockSpec((4, width), whole),
                pl.BlockSpec((block, lanes), spot),
                pl.BlockSpec((block, lanes), spot),
            ]
            + piece_specs
            + [anywhere] * len(earlier),
            out_specs=[
                pl.BlockSpec((block, width), step),
                pl.BlockSpec((block, width), step),
                pl.BlockSpec((block, width), step),
                pl.BlockSpec((block, columns), step),
            ],
            scratch_shapes=[pltpu.VMEM((width, columns), low)],
        ),
        out_shape=[
            jax.ShapeDtypeStruct((rows, width), low),
            jax.ShapeDtypeStruct((rows, width), low),
            jax.ShapeDtypeStruct((rows, width), low),
            jax.ShapeDtypeStruct((rows, columns), low),
        ],
        input_output_aliases={6 + len(pieces) + i: i for i in range(len(earlier))},
        compiler_params=pltpu.CompilerParams(vmem_limit_bytes=kernel_memory),
        cost_estimate=effort(12 * sum(p.shape[0] for p in pieces) / 2048),
        name="project",
    )(place, head, bias, norms, cosine, sine, *pieces, *earlier)


def contract(a, b, da, db):
    return lax.dot_general(a, b, (((da,), (db,)), ((), ())), preferred_element_type=full)


def head_lanes(x, head, pair, head_dim):
    if pair == 1:
        return x
    lane = lax.broadcasted_iota(jnp.int32, x.shape, 1)
    inside = (lane >= head * head_dim) & (lane < (head + 1) * head_dim)
    return jnp.where(inside, x, jnp.zeros_like(x))


def attend_kernel(pair, head_dim, place, qkv_ref, exact_ref, low_ref, lse_ref):
    count, block, lanes3 = qkv_ref.shape
    lanes = lanes3 // 3
    scale = 1.0 / math.sqrt(head_dim)
    s = place[0]
    row = lax.broadcasted_iota(jnp.int32, (block, block), 0)
    column = lax.broadcasted_iota(jnp.int32, (block, block), 1)
    for i in range(count):
        here = i ^ s
        query = qkv_ref[here, :, 0:lanes] * jnp.asarray(scale, low)
        joined = jnp.zeros((block, lanes), full)
        for head in range(pair):
            mine = head_lanes(query, head, pair, head_dim)
            scores = []
            for j in range(i + 1):
                part = contract(mine, qkv_ref[j ^ s, :, lanes : 2 * lanes], 1, 1)
                if j == i:
                    part = jnp.where(column <= row, part, masked_score)
                scores.append(part)
            top = functools.reduce(jnp.maximum, scores)
            top = jnp.max(top, axis=-1, keepdims=True)
            total = None
            update = None
            for j in range(i + 1):
                weights = jnp.exp(scores[j] - top)
                term = jnp.dot(
                    weights.astype(low), qkv_ref[j ^ s, :, 2 * lanes :], preferred_element_type=full
                )
                update = term if update is None else update + term
                total = weights if total is None else total + weights
            total = jnp.sum(total, axis=-1, keepdims=True)
            joined = joined + head_lanes(update / total, head, pair, head_dim)
            lse = jnp.broadcast_to(top + jnp.log(total), (block, 128))
            lse_ref[here, head : head + 1, :] = jnp.transpose(lse)[0:1, :]
        exact_ref[here] = joined
        low_ref[here] = joined.astype(low)


def attend(place, qkv, pair, head_dim):
    count, seqs, block, columns = qkv.shape
    lanes = pair * head_dim
    groups = columns // (3 * lanes)
    spec = lambda width: pl.BlockSpec((count, None, block, width), lambda b, g, place: (0, b, 0, g))
    return pl.pallas_call(
        functools.partial(attend_kernel, pair, head_dim),
        grid_spec=pltpu.PrefetchScalarGridSpec(
            num_scalar_prefetch=1,
            grid=(seqs, groups),
            in_specs=[spec(3 * lanes)],
            out_specs=[
                spec(lanes),
                spec(lanes),
                pl.BlockSpec((count, None, None, pair, block), lambda b, g, place: (0, b, g, 0, 0)),
            ],
        ),
        out_shape=[
            jax.ShapeDtypeStruct((count, seqs, block, groups * lanes), full),
            jax.ShapeDtypeStruct((count, seqs, block, groups * lanes), low),
            jax.ShapeDtypeStruct((count, seqs, groups, pair, block), full),
        ],
        compiler_params=pltpu.CompilerParams(vmem_limit_bytes=kernel_memory),
        cost_estimate=effort(18 * seqs * groups / 2),
        name="attend",
    )(place, qkv)


def attend_back_kernel(pair, head_dim, place, qkv_ref, exact_ref, grad_ref, lse_ref, cos_ref, sin_ref, *refs):
    out_ref, key_ref, value_ref = refs[-3:]
    count, block, lanes3 = qkv_ref.shape
    lanes = lanes3 // 3
    scale = 1.0 / math.sqrt(head_dim)
    s = place[0]
    row = lax.broadcasted_iota(jnp.int32, (block, block), 0)
    column = lax.broadcasted_iota(jnp.int32, (block, block), 1)
    key_ref[...] = jnp.zeros_like(key_ref)
    value_ref[...] = jnp.zeros_like(value_ref)

    def back(total, at):
        kept = total.astype(low).astype(full)
        return turn(kept, cos_ref[at], -sin_ref[at], head_dim).astype(low)

    for i in range(count):
        here = i ^ s
        query = qkv_ref[here, :, 0:lanes] * jnp.asarray(scale, low)
        grad = grad_ref[here]
        product = exact_ref[here] * grad.astype(full)
        joined = jnp.zeros((block, lanes), full)
        for head in range(pair):
            mine = head_lanes(query, head, pair, head_dim)
            mine_grad = head_lanes(grad, head, pair, head_dim)
            delta = jnp.sum(
                jnp.transpose(head_lanes(product, head, pair, head_dim)), axis=0, keepdims=True
            )
            lse = lse_ref[here, head : head + 1, :]
            update = None
            for j in range(i + 1):
                there = j ^ s
                key = qkv_ref[there, :, lanes : 2 * lanes]
                value = qkv_ref[there, :, 2 * lanes :]
                scores = contract(key, mine, 1, 1)
                if j == i:
                    scores = jnp.where(row <= column, scores, masked_score)
                probs = jnp.exp(scores - lse)
                prob_grad = contract(value, mine_grad, 1, 1)
                score_grad = (probs * (prob_grad - delta)).astype(low)
                value_ref[j] += jnp.dot(probs.astype(low), mine_grad, preferred_element_type=full)
                key_ref[j] += jnp.dot(score_grad, mine, preferred_element_type=full)
                term = contract(score_grad, key, 0, 0)
                update = term if update is None else update + term
            joined = joined + head_lanes(update, head, pair, head_dim)
        out_ref[here, :, 0:lanes] = back(joined * scale, i)
    for j in range(count):
        there = j ^ s
        out_ref[there, :, lanes : 2 * lanes] = back(key_ref[j], j)
        out_ref[there, :, 2 * lanes :] = value_ref[j].astype(low)


def attend_back(place, qkv, exact, grad, lse, cosine, sine, pair, head_dim, wait):
    count, seqs, block, columns = qkv.shape
    lanes = pair * head_dim
    groups = columns // (3 * lanes)
    spec = lambda width: pl.BlockSpec((count, None, block, width), lambda b, g, place: (0, b, 0, g))
    table = pl.BlockSpec((count, block, lanes), lambda b, g, place: (0, 0, 0))
    return pl.pallas_call(
        functools.partial(attend_back_kernel, pair, head_dim),
        grid_spec=pltpu.PrefetchScalarGridSpec(
            num_scalar_prefetch=1,
            grid=(seqs, groups),
            in_specs=[
                spec(3 * lanes),
                spec(lanes),
                spec(lanes),
                pl.BlockSpec((count, None, None, pair, block), lambda b, g, place: (0, b, g, 0, 0)),
                table,
                table,
            ]
            + [anywhere] * len(wait),
            out_specs=spec(3 * lanes),
            scratch_shapes=[
                pltpu.VMEM((count, block, lanes), full),
                pltpu.VMEM((count, block, lanes), full),
            ],
        ),
        out_shape=jax.ShapeDtypeStruct(qkv.shape, low),
        compiler_params=pltpu.CompilerParams(vmem_limit_bytes=kernel_memory),
        cost_estimate=effort(33 * seqs * groups / 2),
        name="attend_back",
    )(place, qkv, exact, grad, lse, cosine, sine, *wait)


def expand_kernel(x_ref, weight_ref, bias_ref, *refs):
    active_ref, slope_ref = refs[-2:]
    hidden = jnp.dot(x_ref[...], weight_ref[...], preferred_element_type=full) + bias_ref[...]
    tail = 0.5 * (1.0 + lax.erf(hidden * np.float32(math.sqrt(0.5))))
    bell = jnp.exp(-0.5 * hidden * hidden) * np.float32(1.0 / math.sqrt(2.0 * math.pi))
    active_ref[...] = (hidden * tail).astype(low)
    slope_ref[...] = (tail + hidden * bell).astype(low)


def expand(x, weight, bias, block, wait):
    rows, width = x.shape
    columns = weight.shape[1]
    whole = lambda i: (0, 0)
    step = lambda i: (i, 0)
    return pl.pallas_call(
        expand_kernel,
        grid=(rows // block,),
        in_specs=[
            pl.BlockSpec((block, width), step),
            pl.BlockSpec((width, columns), whole),
            pl.BlockSpec((1, columns), whole),
        ]
        + [anywhere] * len(wait),
        out_specs=[pl.BlockSpec((block, columns), step), pl.BlockSpec((block, columns), step)],
        out_shape=[jax.ShapeDtypeStruct((rows, columns), low)] * 2,
        compiler_params=pltpu.CompilerParams(vmem_limit_bytes=kernel_memory),
        cost_estimate=effort(12 * rows / 2048),
        name="expand",
    )(x, weight, bias, *wait)


def turnabout_kernel(stacked, count, units, attended_ref, active_ref, slope_ref, back_ref, *refs):
    pieces, parts = refs[:count], refs[count:-6]
    cot_ref, attended_grad_ref, hidden_grad_ref, sum_ref, down_ref, out_ref = refs[-6:]
    block, width = cot_ref.shape
    step = pl.program_id(0)

    @pl.when(step == 0)
    def _():
        down_ref[...] = back_ref[:, :units, :].reshape(down_ref.shape)
        out_ref[...] = back_ref[:, units:, :].reshape(out_ref.shape)

    down, out = down_ref[...], out_ref[...]
    part = jnp.dot(attended_ref[...], out, preferred_element_type=full)
    part = part + jnp.dot(active_ref[...], down, preferred_element_type=full)
    part = part.astype(low)
    if stacked:
        cot_ref[...] = pieces[0][...]
        parts[0][...] = part
    else:
        for k, ref in enumerate(parts):

            @pl.when(step == k)
            def _(ref=ref):
                ref[...] = part

        first = 0
        for piece in pieces:
            rows = piece.shape[0]
            inside = first % block

            @pl.when(step == first // block)
            def _(piece=piece, inside=inside, rows=rows):
                cot_ref[inside : inside + rows, :] = piece[...]

            first += rows
    cot = cot_ref[...]
    attended_grad_ref[...] = contract(cot, out, 1, 1).astype(low)
    hidden = (contract(cot, down, 1, 1) * slope_ref[...].astype(full)).astype(low)
    hidden_grad_ref[...] = hidden
    total = jnp.sum(hidden.astype(full), axis=0, keepdims=True)

    @pl.when(step == 0)
    def _():
        sum_ref[...] = total

    @pl.when(step > 0)
    def _():
        sum_ref[...] += total


def turnabout(attended, active, slope, back_weights, pieces, block, units):
    stacked = len(pieces) == 1
    rows, span = attended.shape
    columns, width = active.shape[1], back_weights.shape[2]
    whole = lambda i: (0, 0)
    step = lambda i: (i, 0)
    if stacked:
        piece_specs = [pl.BlockSpec((block, width), step)]
        part_specs = piece_specs
        part_shapes = [jax.ShapeDtypeStruct((rows, width), low)]
    else:
        piece_specs = [pl.BlockSpec(p.shape, whole) for p in pieces]
        part_specs = [pl.BlockSpec((block, width), whole)] * (rows // block)
        part_shapes = [jax.ShapeDtypeStruct((block, width), low)] * (rows // block)
    *parts, cot, attended_grad, hidden_grad, total = pl.pallas_call(
        functools.partial(turnabout_kernel, stacked, len(pieces), units),
        grid=(rows // block,),
        in_specs=[
            pl.BlockSpec((block, span), step),
            pl.BlockSpec((block, columns), step),
            pl.BlockSpec((block, columns), step),
            pl.BlockSpec(back_weights.shape, lambda i: (0, 0, 0)),
        ]
        + piece_specs,
        out_specs=part_specs
        + [
            pl.BlockSpec((block, width), step),
            pl.BlockSpec((block, span), step),
            pl.BlockSpec((block, columns), step),
            pl.BlockSpec((1, columns), whole),
        ],
        out_shape=part_shapes
        + [
            jax.ShapeDtypeStruct((rows, width), low),
            jax.ShapeDtypeStruct((rows, span), low),
            jax.ShapeDtypeStruct((rows, columns), low),
            jax.ShapeDtypeStruct((1, columns), full),
        ],
        scratch_shapes=[pltpu.VMEM((columns, width), low), pltpu.VMEM((span, width), low)],
        compiler_params=pltpu.CompilerParams(vmem_limit_bytes=kernel_memory),
        cost_estimate=effort(14 * rows / 2048),
        name="turnabout",
    )(attended, active, slope, back_weights, *pieces)
    return parts, cot, attended_grad, hidden_grad, total


def outer_kernel(count, *refs):
    out_ref = refs[2 * count]
    for which in range(count):

        @pl.when(pl.program_id(0) == which)
        def _(which=which):
            got = contract(refs[2 * which][...], refs[2 * which + 1][...], 0, 0)
            out_ref[...] = got.astype(low).reshape(out_ref.shape)


def outer(pairs, parts, halves):
    count = len(pairs)
    rows, columns = pairs[0][0].shape
    width = pairs[0][1].shape[1]
    units = columns // parts
    specs, arrays = [], []
    for which, (a, b) in enumerate(pairs):
        mine = lambda w, h, which=which: (0, jnp.where(w == which, h, jnp.where(w < which, 0, halves - 1)))
        specs += [pl.BlockSpec((rows, columns // halves), mine), pl.BlockSpec((rows, width), lambda w, h: (0, 0))]
        arrays += [a, b]
    return pl.pallas_call(
        functools.partial(outer_kernel, count),
        grid=(count, halves),
        in_specs=specs,
        out_specs=pl.BlockSpec((parts // halves, units, width), lambda w, h: (h, w, 0)),
        out_shape=jax.ShapeDtypeStruct((parts, count * units, width), low),
        compiler_params=pltpu.CompilerParams(vmem_limit_bytes=kernel_memory),
        cost_estimate=effort(5 * count * rows * columns * width / 2**31),
        name="outer",
    )(*arrays)


def hand_kernel(count, moves, place, *refs):
    out = refs[count]
    for k in range(count):
        rank = place[0] ^ k
        for source, target, stride, size in moves:
            piece = refs[k][:, source : source + size].astype(full)
            if size % 128 == 0 and stride % 128 == 0:
                out[:, pl.ds(pl.multiple_of(target + rank * stride, 128), size)] = piece
            else:
                for r in range(count):

                    @pl.when(rank == r)
                    def _(r=r, piece=piece, target=target, stride=stride, size=size):
                        out[:, target + r * stride : target + r * stride + size] = piece


def hand(place, pieces, moves):
    count = len(pieces)
    rows, columns = pieces[0].shape
    vmem = pl.BlockSpec(memory_space=pltpu.VMEM)
    return pl.pallas_call(
        functools.partial(hand_kernel, count, moves),
        in_specs=[pl.BlockSpec(memory_space=pltpu.SMEM)] + [vmem] * count,
        out_specs=vmem,
        out_shape=jax.ShapeDtypeStruct((rows, count * columns), full),
        compiler_params=pltpu.CompilerParams(vmem_limit_bytes=kernel_memory),
        name="hand",
    )(place, *pieces)


def finish_kernel(x_ref, cot_ref, own_ref, first_ref, second_ref, *refs):
    unit, rstd = normalised(x_ref[...].astype(full))
    total = own_ref[...].astype(full) + first_ref[...].astype(full) + second_ref[...].astype(full)
    shift = jnp.mean(total, axis=-1, keepdims=True)
    tilt = jnp.mean(total * unit, axis=-1, keepdims=True)
    refs[-1][...] = (cot_ref[...].astype(full) + rstd * (total - shift - unit * tilt)).astype(low)


def finish(x, cot, own, first, second, wait):
    rows, width = x.shape
    block = rows // 4 if rows % 64 == 0 else rows
    spec = pl.BlockSpec((block, width), lambda i: (i, 0))
    return pl.pallas_call(
        finish_kernel,
        grid=(rows // block,),
        in_specs=[spec] * 5 + [anywhere] * len(wait),
        out_specs=spec,
        out_shape=jax.ShapeDtypeStruct((rows, width), low),
        compiler_params=pltpu.CompilerParams(vmem_limit_bytes=kernel_memory),
        cost_estimate=effort(3 * rows / 512),
        name="finish",
    )(x, cot, own, first, second, *wait)


def unproject_kernel(x_ref, mixed_ref, hidden_ref, in_ref, up_ref, norms_ref, *refs):
    out_ref, sums_ref = refs[-2:]
    unit, _ = normalised(x_ref[...].astype(full))
    width, columns = x_ref.shape[1], mixed_ref.shape[1]
    in_weight = in_ref[:, : width // in_ref.shape[0], :columns].reshape(width, columns)
    attn = contract(mixed_ref[...], in_weight, 1, 1)
    ff = contract(hidden_ref[...], up_ref[...], 1, 1)
    out_ref[...] = (attn * norms_ref[0:1, :] + ff * norms_ref[2:3, :]).astype(low)
    sums = [attn * unit, attn, ff * unit, ff]
    sums = jnp.concatenate([jnp.sum(a, axis=0, keepdims=True) for a in sums], 0)

    @pl.when(pl.program_id(0) == 0)
    def _():
        sums_ref[...] = sums

    @pl.when(pl.program_id(0) > 0)
    def _():
        sums_ref[...] += sums


def unproject(x, mixed, hidden, in_weight, up_weight, norms, block, first, count, wait):
    rows, width = count * block, x.shape[1]
    whole = lambda i: (0, 0)
    step = lambda i: (i + first, 0)
    here = lambda i: (i, 0)
    return pl.pallas_call(
        unproject_kernel,
        grid=(rows // block,),
        in_specs=[
            pl.BlockSpec((block, width), step),
            pl.BlockSpec((block, mixed.shape[1]), step),
            pl.BlockSpec((block, hidden.shape[1]), step),
            pl.BlockSpec(in_weight.shape, lambda i: (0, 0, 0)),
            pl.BlockSpec(up_weight.shape, whole),
            pl.BlockSpec((4, width), whole),
        ]
        + [anywhere] * len(wait),
        out_specs=[pl.BlockSpec((block, width), here), pl.BlockSpec((4, width), whole)],
        out_shape=[
            jax.ShapeDtypeStruct((rows, width), low),
            jax.ShapeDtypeStruct((4, width), full),
        ],
        compiler_params=pltpu.CompilerParams(vmem_limit_bytes=kernel_memory),
        cost_estimate=effort(18 * rows / 2048),
        name="unproject",
    )(x, mixed, hidden, in_weight, up_weight, norms, *wait)


def reduce_steps(at, far, near):
    if at.seq != 4:
        got = [at.seq_swap(a, k + 1) for k, a in enumerate(near())]
        return [], got + [at.seq_swap(far, at.seq - 1)]
    first = at.seq_reduce_far(far)
    return first, list(at.seq_reduce_near(near(), first))


def on_device(
    tokens,
    input_weight,
    input_bias,
    output_weight,
    output_bias,
    up_weight,
    up_bias,
    down_weight,
    down_bias,
    attention_gain,
    attention_shift,
    feedforward_gain,
    feedforward_shift,
    cotangent,
):
    at = Layout()
    dp, seq, rank = at.dp, at.seq, at.rank
    seqs, block, width = tokens.shape
    shard = input_weight.shape[0]
    units = down_weight.shape[0]
    head_dim = width // HEADS
    heads = HEADS // seq
    pair = 2 if heads % 2 == 0 else 1
    groups = heads // pair
    lanes = pair * head_dim
    span = heads * head_dim
    place = rank.astype(jnp.int32).reshape(1)

    vectors = (input_bias, output_bias, up_bias, down_bias, attention_gain, attention_shift, feedforward_gain, feedforward_shift)
    dealt = deal(place, input_weight, up_weight, vectors, seq, groups, units)
    head_rows, up_rows = gather_heads(
        place, [dealt[0]] + [at.seq_swap(dealt[k], k) for k in range(1, seq)], shard
    )
    out_rows = at.to_heads(output_weight)
    tokens_all = at.seq_gather(tokens)
    head_all = at.dp_gather(head_rows)
    up_all = at.dp_gather(up_rows).reshape(width, dp * units)
    back_all = at.dp_gather(join(down_weight, out_rows, (up_rows,)))

    gathered = head_all[:, seq * shard :, :].reshape(dp, seq, 8, 3 * span)
    bias_in, bias_out, bias_up, bias_down, gain_attn, shift_attn, gain_ff, shift_ff = (
        gathered[:, :, i, : v.shape[0]].reshape(-1).astype(full) for i, v in enumerate(vectors)
    )
    norms = jnp.stack([gain_attn, shift_attn, gain_ff, shift_ff], 0)

    rows = seq * seqs * block
    pieces = [p.reshape(-1, width) for p in tokens_all]
    in_bias_mine = jnp.swapaxes(
        pick(bias_in.reshape(3, seq, groups, lanes), rank, 1), 0, 1
    ).reshape(1, 3 * span)
    up_bias_mine = pick(bias_up.reshape(dp, seq, units), rank, 1).reshape(1, dp * units)

    cos_table, sin_table = rotary_tables(seq * block, lanes, head_dim)

    def run(pieces, *more):
        return project(
            place, pieces, head_all, in_bias_mine, norms, jnp.asarray(cos_table), jnp.asarray(sin_table),
            block, seqs, lanes, head_dim, seq * shard, rows, *more,
        )

    if seq == 4 and seqs == 1:
        earlier = run(pieces[:3])
        cot_near = at.seq_gather_near(after(cotangent, earlier[3]))
        x, normed_attn, normed_ff, qkv = run(pieces[3:], 3, tuple(earlier))
    else:
        x, normed_attn, normed_ff, qkv = run([jnp.concatenate(pieces, 0)])
        cot_near = at.seq_gather_near(cotangent)
    qkv = qkv.reshape(seq, seqs, block, 3 * span)
    exact, attended, lse = attend(place, qkv, pair, head_dim)
    attended = attended.reshape(rows, span)
    cot_all = at.seq_gather_far(cot_near, attended)

    active, slope = expand(normed_ff, up_all, up_bias_mine, block, (attended,))

    pieces = [p.reshape(-1, width) for p in cot_all]
    if seq != 4 or seqs != 1:
        pieces = [jnp.concatenate(pieces, 0)]
    out_part, cot, attended_grad, hidden_grad, up_bias_sum = turnabout(
        attended, active, slope, back_all, pieces, block, units
    )
    if len(out_part) == 1:
        out_part = out_part[0].reshape(seq, seqs * block, width)
    out_near = [at.seq_swap(out_part[k], k) for k in range(1, seq)]

    out_grad = lax.optimization_barrier(contract(attended, cot, 0, 0).astype(low))
    out_grads = at.dp_reduce(out_grad.reshape(dp, shard, width))
    if dp * units == width:
        unit_grads = outer([(active, cot), (normed_ff, hidden_grad)], dp, 2)
    else:
        down_grad = contract(active, cot, 0, 0).astype(low)
        up_grad = contract(normed_ff, hidden_grad, 0, 0).astype(low)
        unit_grads = jnp.concatenate(
            [down_grad.reshape(dp, units, width), up_grad.reshape(dp, seq * shard * dp * units // width, width)], 1
        )
    back_wait = (unit_grads, out_grad)
    unit_sum_grads = at.dp_reduce(unit_grads)

    tables = [jnp.asarray(t.reshape(seq, block, lanes)) for t in (cos_table, sin_table)]
    mixed_grad = attend_back(
        place, qkv, exact, attended_grad.reshape(seq, seqs, block, span), lse, *tables, pair, head_dim, back_wait
    )
    mixed_grad = mixed_grad.reshape(rows, 3 * span)
    in_grad = lax.optimization_barrier(contract(normed_attn, mixed_grad, 0, 0).astype(low))
    in_grad = in_grad.reshape(dp, seq * shard, 3 * span)
    wait = (out_grads,)
    last = (seq - 1) * seqs
    weights = (head_all, up_all, norms)
    far_grad, far_sums = unproject(x, mixed_grad, hidden_grad, *weights, block, last, seqs, wait)
    in_ready = after_big(in_grad, unit_sum_grads)
    in_grads = at.dp_reduce(in_ready)
    near_grad, near_sums = unproject(x, mixed_grad, hidden_grad, *weights, block, seqs, last - seqs, (far_grad, in_ready))
    own_grad, own_sums = unproject(x, mixed_grad, hidden_grad, *weights, block, 0, seqs, (near_grad,))
    norm_sums = far_sums + near_sums + own_sums
    near_grad = near_grad.reshape(seq - 2, seqs, block, width)
    _, unit_near = reduce_steps(
        at, far_grad.reshape(seqs, block, width), lambda: [near_grad[k] for k in range(seq - 2)]
    )
    out_sum = out_part[0].astype(full) + sum(a.astype(full) for a in out_near)
    output = tokens.astype(full) + out_sum.reshape(tokens.shape) + (bias_out + bias_down)
    output = output.astype(low)
    in_bias_sum = jnp.sum(mixed_grad.astype(full), axis=0).reshape(groups, 3, lanes)
    in_bias_sum = jnp.swapaxes(in_bias_sum, 0, 1).reshape(3, 1, span)
    in_bias_sum = lax.dynamic_update_slice_in_dim(jnp.zeros((3, seq, span), full), in_bias_sum, rank, 1)
    up_bias_sum = up_bias_sum.reshape(dp, 1, units)
    up_bias_sum = lax.dynamic_update_slice_in_dim(jnp.zeros((dp, seq, units), full), up_bias_sum, rank, 1)
    out_bias_sum = jnp.sum(cotangent.astype(full), axis=(0, 1))
    in_bias_sum = in_bias_sum.reshape(3 * width)
    small = [
        in_bias_sum[: 2 * width],
        in_bias_sum[2 * width :],
        out_bias_sum,
        up_bias_sum,
        norm_sums[0],
        norm_sums[1],
        norm_sums[2],
        norm_sums[3],
    ]
    small = jnp.concatenate([v.reshape(dp, seq, -1) for v in small], 2)
    lengths = [3 * shard - shard, shard, shard, units, shard, shard, shard, shard]
    edges = np.cumsum([0] + lengths)

    down_final = unit_sum_grads[:units].astype(full)
    up_final = unit_sum_grads[units:].reshape(seq, shard, dp * units)
    up_moves = [(d * units, d * seq * units, units, units) for d in range(dp)]
    up_final = hand(place, at.seq_exchange(lambda spot: pick(up_final, spot, 0)), up_moves)
    out_final = at.from_heads(out_grads).astype(full)
    in_split = in_grads.reshape(seq, shard, 3 * span)
    in_moves = [
        ((g * 3 + kind) * lanes, kind * width + g * lanes, span, lanes) for g in range(groups) for kind in range(3)
    ]
    in_final = hand(place, at.seq_exchange(lambda spot: pick(in_split, spot, 0)), in_moves)
    total = at.small_reduce(small)
    flat = [a.reshape(-1, width) for a in (tokens, cotangent, own_grad)]
    if len(unit_near) == 2:
        others = [a.reshape(-1, width) for a in unit_near]
    else:
        others = [sum(a.astype(full) for a in unit_near).reshape(-1, width), jnp.zeros_like(flat[0])]
    token_grad = finish(*flat, *others, (output, total, up_final)).reshape(seqs, block, width)
    (query_key_bias, value_bias, out_bias, up_bias_grad, *norm_grads) = [
        total[edges[i] : edges[i + 1]] for i in range(8)
    ]
    return (
        output,
        token_grad,
        in_final,
        query_key_bias,
        value_bias,
        out_final,
        out_bias,
        up_final,
        up_bias_grad,
        down_final,
        out_bias,
        *norm_grads,
    )


def solution(mesh):
    rows = P(("dp", "seq"), None)
    flat = P(("dp", "seq"))
    held = P("dp", "seq", None)
    return jax.shard_map(
        on_device,
        mesh=mesh,
        in_specs=(held, rows, flat, rows, flat, rows, flat, rows, flat, flat, flat, flat, flat, held),
        out_specs=(held, held, rows, flat, flat, rows, flat, rows, flat, rows, flat, flat, flat, flat, flat),
        check_vma=False,
    )
```

profile of v0, /device:TPU:0, one launch (start us, length us, event | category | flops | bytes accessed | tf_op | source)
XLA Modules:
  0.0 304.2 jit_solution(7909166781778396482)
XLA Ops:
  7.2 2.0 deal.1
  9.2 2.9 collective-permute-start
  12.1 1.5 collective-permute-start.1
  13.7 3.7 %collective-permute-done.refs_1_ = bf16[80,1024]{1,0:T(8,128)(2,1)S(1)} collective-permute-done((bf16[80,1024]{1,0:T(8,128)(2,1)}, bf16[80,1024]{1,0:T(8,128)(2,1)S(1)}, u32[]{:S(2)}, u32[]{:S(2)}) %collective-permute-start) | collective-permute-done | bytes 163872 | tf_op jit(solution)/shard_map/ppermute | solution.py:278
  17.4 4.1 %collective-permute-done.1.refs_2_ = bf16[80,1024]{1,0:T(8,128)(2,1)S(1)} collective-permute-done((bf16[80,1024]{1,0:T(8,128)(2,1)}, bf16[80,1024]{1,0:T(8,128)(2,1)S(1)}, u32[]{:S(2)}, u32[]{:S(2)}) %collective-permute-start.1) | collective-permute-done | bytes 163872 | tf_op jit(solution)/shard_map/ppermute | solution.py:278
  22.2 2.0 gather_heads.1
  27.2 1.5 collective-permute-start.7
  29.3 1.7 join.1
  31.1 18.8 %collective-permute-done.3.x_ref = bf16[1,512,1024]{2,1,0:T(8,128)(2,1)S(1)} collective-permute-done((bf16[1,512,1024]{2,1,0:T(8,128)(2,1)}, bf16[1,512,1024]{2,1,0:T(8,128)(2,1)S(1)}, u32[]{:S(2)}, u32[]{:S(2)}) %collective-permute-start.3) | collective-permute-done | bytes 1048608 | tf_op jit(solution)/shard_map/ppermute | solution.py:278
  51.8 2.2 cut.2
  55.4 1.6 collective-permute-start.6
  60.0 10.4 %project.2 = (bf16[2048,1024]{1,0:T(8,128)(2,1)}, bf16[2048,1024]{1,0:T(8,128)(2,1)}, bf16[2048,1024]{1,0:T(8,128)(2,1)}, bf16[2048,768]{1,0:T(8,128)(2,1)}) custom-call(s32[1]{0:T(128)} %bitcast.place, bf16[8,160,768]{2,1,0:T(8,128)(2,1)} %bitcast.110, f32[1,768]{1,0:T(1,128)} %reshape.227.bias_ref, f32[4,1024]{1,0:T(4,128)} %maximum_convert_fusion.norms_ref, ...), custom_call_target="tpu_custom_call" | custom-call | flops 9900000256 | bytes 1 | tf_op jit(solution)/shard_map/project/pallas_call | solution.py:443
  70.5 2.3 after.1
  72.8 1.7 collective-permute-start.9
  76.0 5.4 %project.3 = (bf16[2048,1024]{1,0:T(8,128)(2,1)}, bf16[2048,1024]{1,0:T(8,128)(2,1)}, bf16[2048,1024]{1,0:T(8,128)(2,1)}, bf16[2048,768]{1,0:T(8,128)(2,1)}) custom-call(s32[1]{0:T(128)} %bitcast.place, bf16[8,160,768]{2,1,0:T(8,128)(2,1)} %bitcast.111, ...), custom_call_target="tpu_custom_call", output_to_operand_aliasing={{0}: (8, {}), {1}: (9, {}), {2}: (10, {}), {3}: (11, {})} | custom-call | flops 3300000000 | bytes 1 | tf_op jit(solution)/shard_map/project/pallas_call | solution.py:443
  81.5 18.6 %attend.1 = (f32[4,1,512,256]{3,2,1,0:T(8,128)}, bf16[4,1,512,256]{3,2,1,0:T(8,128)(2,1)}, f32[4,1,2,2,512]{4,3,2,1,0:T(2,128)}) custom-call(s32[1]{0:T(128)} %bitcast.place, bf16[4,1,512,768]{3,2,1,0:T(8,128)(2,1)} %bitcast.101), custom_call_target="tpu_custom_call" | custom-call | flops 19800000512 | bytes 1 | tf_op jit(solution)/shard_map/attend/pallas_call | solution.py:533
  101.4 2.2 cut.3
  104.1 1.9 collective-permute-start.11
  106.0 11.3 %expand.1 = (bf16[2048,1024]{1,0:T(8,128)(2,1)}, bf16[2048,1024]{1,0:T(8,128)(2,1)}) custom-call(bf16[2048,1024]{1,0:T(8,128)(2,1)} %get-tuple-element.65.x_ref.refs_2_, bf16[1024,1024]{1,0:T(8,128)(2,1)} %all-gather.9.cloned.1.call-done.weight_ref.up_ref, f32[1,1024]{1,0:T(1,128)} %fusion.9.bias_ref, bf16[2048,256]{1,0:T(8,128)(2,1)} %bitcast.120), custom_call_target="tpu_custom_call" | custom-call | flops 13200000000 | bytes 1 | tf_op jit(solution)/shard_map/expand/pallas_call | solution.py:654
  117.3 1.9 all-gather.11.cloned.1.call-done
  120.1 22.7 %turnabout.1 = (bf16[512,1024]{1,0:T(8,128)(2,1)}, bf16[512,1024]{1,0:T(8,128)(2,1)}, bf16[512,1024]{1,0:T(8,128)(2,1)}, bf16[512,1024]{1,0:T(8,128)(2,1)}, bf16...) custom-call(bf16[2048,256]{1,0:T(8,128)(2,1)} %bitcast.121, ...), custom_call_target="tpu_custom_call" | custom-call | flops 15399999488 | bytes 1 | tf_op jit(solution)/shard_map/turnabout/pallas_call | solution.py:735
  142.8 4.3 %convolution_convert_fusion.1.refs_1_ = bf16[256,1024]{1,0:T(8,128)(2,1)} fusion(bf16[2048,256]{1,0:T(8,128)(2,1)S(1)} %bitcast.122, bf16[2048,1024]{1,0:T(8,128)(2,1)} %get-tuple-element.79.refs_1_), kind=kOutput, calls=%fused_computation.6 | convolution fusion | flops 1074003968 | bytes 5767168 | tf_op jit(solution)/shard_map/dot_general | solution.py:479
  147.2 15.4 %outer.1.refs_0_ = bf16[8,256,1024]{2,1,0:T(8,128)(2,1)} custom-call(bf16[2048,1024]{1,0:T(8,128)(2,1)} %get-tuple-element.67.active_ref.refs_0_, bf16[2048,1024]{1,0:T(8,128)(2,1)} %get-tuple-element.79.refs_1_, bf16[2048,1024]{1,0:T(8,128)(2,1)} %get-tuple-element.65.x_ref.refs_2_, bf16[2048,1024]{1,0:T(8,128)(2,1)} %get-tuple-element.80.refs_3_.hidden_ref), custom_call_target="tpu_custom_call" | custom-call | flops 11000000512 | bytes 1 | tf_op jit(solution)/shard_map/outer/pallas_call | solution.py:787
  164.2 1.5 collective-permute-start.12
  165.6 1.4 collective-permute-start.13
  167.7 33.5 %attend_back.1 = bf16[4,1,512,768]{3,2,1,0:T(8,128)(2,1)} custom-call(s32[1]{0:T(128)} %bitcast.place, bf16[4,1,512,768]{3,2,1,0:T(8,128)(2,1)} %bitcast.102, f32[4,1,512,256]{3,2,1,0:T(8,128)} %get-tuple-element.76.exact_ref, bf16[4,1,512,256]{3,2,1,0:T(8,128)(2,1)} %bitcast.150, f32[4,1,2,2,512]{4,3,2,1,0:T(2,128)} %get-tuple-element.78.lse_ref, ...), custom_call_target="tpu_custom_call" | custom-call | flops 36300001280 | bytes 1 | tf_op jit(solution)/shard_map/attend_back/pallas_call | solution.py:613
  201.2 6.7 %convolution_convert_fusion = bf16[1024,768]{1,0:T(8,128)(2,1)} fusion(bf16[2048,1024]{1,0:T(8,128)(2,1)S(1)} %copy-done.1, bf16[2048,768]{1,0:T(8,128)(2,1)} %bitcast.105), kind=kOutput, calls=%fused_computation.5 | convolution fusion | flops 3222011904 | bytes 8912896 | tf_op jit(solution)/shard_map/dot_general | solution.py:479
  208.8 1.5 collective-permute-start.32
  210.3 6.6 %unproject.3 = (bf16[512,1024]{1,0:T(8,128)(2,1)}, f32[4,1024]{1,0:T(4,128)}) custom-call(bf16[2048,1024]{1,0:T(8,128)(2,1)} %get-tuple-element.75.x_ref, bf16[2048,768]{1,0:T(8,128)(2,1)} %bitcast.106, bf16[2048,1024]{1,0:T(8,128)(2,1)} %get-tuple-element.80.refs_3_.hidden_ref, bf16[8,160,768]{2,1,0:T(8,128)(2,1)} %bitcast.112, ...), custom_call_target="tpu_custom_call" | custom-call | flops 4950000128 | bytes 1 | tf_op jit(solution)/shard_map/unproject/pallas_call | solution.py:878
  216.9 2.4 fusion.14
  219.3 3.5 %collective-permute-start.17 = (bf16[1,256,1024]{2,1,0:T(8,128)(2,1)}, bf16[1,256,1024]{2,1,0:T(8,128)(2,1)}, u32[]{:S(2)}, u32[]{:S(2)}) collective-permute-start(bf16[1,256,1024]{2,1,0:T(8,128)(2,1)} %get-tuple-element.103), channel_id=1, source_target_pairs={{0,1},{1,0},{2,3},{3,2},{4,5},{5,4},{6,7},{7,6},{8,9},{9,8},{10,11... | collective-permute-start | bytes 1572872 | tf_op jit(solution)/shard_map/ppermute | solution.py:278
  222.8 1.9 collective-permute-start.15
  224.7 2.2 fusion.1.refs_0_
  227.6 1.9 reduce-scatter.6.cloned.1.call-done
  229.5 9.0 %unproject.4 = (bf16[1024,1024]{1,0:T(8,128)(2,1)}, f32[4,1024]{1,0:T(4,128)}) custom-call(bf16[2048,1024]{1,0:T(8,128)(2,1)} %get-tuple-element.75.x_ref, bf16[2048,768]{1,0:T(8,128)(2,1)} %bitcast.107, bf16[2048,1024]{1,0:T(8,128)(2,1)} %get-tuple-element.80.refs_3_.hidden_ref, bf16[8,160,768]{2,1,0:T(8,128)(2,1)} %bitcast.113, ...), custom_call_target="tpu_custom_call" | custom-call | flops 9900000256 | bytes 1 | tf_op jit(solution)/shard_map/unproject/pallas_call | solution.py:878
  238.6 6.6 %unproject.5 = (bf16[512,1024]{1,0:T(8,128)(2,1)}, f32[4,1024]{1,0:T(4,128)}) custom-call(bf16[2048,1024]{1,0:T(8,128)(2,1)} %get-tuple-element.75.x_ref, bf16[2048,768]{1,0:T(8,128)(2,1)} %bitcast.108, bf16[2048,1024]{1,0:T(8,128)(2,1)} %get-tuple-element.80.refs_3_.hidden_ref, bf16[8,160,768]{2,1,0:T(8,128)(2,1)} %bitcast.114, ...), custom_call_target="tpu_custom_call" | custom-call | flops 4950000128 | bytes 1 | tf_op jit(solution)/shard_map/unproject/pallas_call | solution.py:878
  246.7 1.6 collective-permute-start.19
  248.2 1.5 collective-permute-start.21
  251.6 1.6 collective-permute-start.16
  256.6 4.5 %collective-permute-start.25 = (f32[384]{0:T(512)S(1)}, f32[384]{0:T(512)S(1)}, u32[]{:S(2)}, u32[]{:S(2)}) collective-permute-start(f32[384]{0:T(512)S(1)} %get-tuple-element.98), channel_id=1, source_target_pairs={{0,24},{4,28},{8,0},{12,4},{16,8},{20,12},{24,16},{28,20},{1,25},{... | collective-permute-start | bytes 4616 | tf_op jit(solution)/shard_map/ppermute | solution.py:334
  263.4 1.5 collective-permute-start.27
  268.0 11.6 %collective-permute-done.28.refs_3_ = bf16[32,1024]{1,0:T(8,128)(2,1)S(1)} collective-permute-done((bf16[32,1024]{1,0:T(8,128)(2,1)S(1)}, bf16[32,1024]{1,0:T(8,128)(2,1)S(1)}, u32[]{:S(2)}, u32[]{:S(2)}) %collective-permute-start.28) | collective-permute-done | bytes 65568 | tf_op jit(solution)/shard_map/ppermute | solution.py:278
  279.6 2.3 collective-permute-done.27.refs_2_
  282.6 1.8 hand.2.refs_2_
  284.4 1.5 dynamic-slice_bitcast_fusion.4
  287.3 1.7 collective-permute-start.30
  289.4 5.0 %finish.1 = bf16[512,1024]{1,0:T(8,128)(2,1)} custom-call(bf16[512,1024]{1,0:T(8,128)(2,1)} %bitcast.128, bf16[512,1024]{1,0:T(8,128)(2,1)} %bitcast.104, bf16[512,1024]{1,0:T(8,128)(2,1)} %get-tuple-element.84.own_ref, bf16[512,1024]{1,0:T(8,128)(2,1)} %bitcast.37.first_ref, bf16[512,1024]{1,0:T(8,128)(2,1)} %bitcast.39.second_ref, ...), custom_call_target="tpu_custom_call" | custom-call | flops 3300000000 | bytes 1 | tf_op jit(solution)/shard_map/finish/pallas_call | solution.py:841
  295.0 1.7 hand.3
  (188 shorter events, 34.4 us)
Async XLA Ops:
  7.2 49.8 %all-gather.7.cloned.1.call-start = ((), (), s32[]{:S(2)}) async-start(), calls=%async_computation.6 | async-start | bytes 2211840 | tf_op jit(solution)/shard_map/all_gather | solution.py:354
  9.2 8.2 %collective-permute-start = (bf16[80,1024]{1,0:T(8,128)(2,1)}, bf16[80,1024]{1,0:T(8,128)(2,1)S(1)}, u32[]{:S(2)}, u32[]{:S(2)}) collective-permute-start(bf16[80,1024]{1,0:T(8,128)(2,1)} %get-tuple-element.53), channel_id=1, source_target_pairs={{0,1},{1,0},{2,3},{3,2},{4,5},{5,4},{6,7},{7,6},{8,9},{9,8},{10,11... | collective-permute-start | bytes 491528 | tf_op jit(solution)/shard_map/ppermute | solution.py:278
  12.1 9.4 %collective-permute-start.1 = (bf16[80,1024]{1,0:T(8,128)(2,1)}, bf16[80,1024]{1,0:T(8,128)(2,1)S(1)}, u32[]{:S(2)}, u32[]{:S(2)}) collective-permute-start(bf16[80,1024]{1,0:T(8,128)(2,1)} %get-tuple-element.54), channel_id=1, source_target_pairs={{0,2},{1,3},{2,0},{3,1},{4,6},{5,7},{6,4},{7,5},{8,10},{9,11},{10,... | collective-permute-start | bytes 491528 | tf_op jit(solution)/shard_map/ppermute | solution.py:278
  13.7 7.9 %collective-permute-start.2 = (bf16[80,1024]{1,0:T(8,128)(2,1)}, bf16[80,1024]{1,0:T(8,128)(2,1)S(1)}, u32[]{:S(2)}, u32[]{:S(2)}) collective-permute-start(bf16[80,1024]{1,0:T(8,128)(2,1)} %get-tuple-element.55), channel_id=1, source_target_pairs={{0,3},{1,2},{2,1},{3,0},{4,7},{5,6},{6,5},{7,4},{8,11},{9,10},{10,... | collective-permute-start | bytes 491528 | tf_op jit(solution)/shard_map/ppermute | solution.py:278
  24.3 81.7 %all-gather.9.cloned.1.call-start = ((), (), s32[]{:S(2)}) async-start(), calls=%async_computation.7 | async-start | bytes 2359296 | tf_op jit(solution)/shard_map/all_gather | solution.py:354
  25.0 94.1 %all-gather.11.cloned.1.call-start = ((), (), s32[]{:S(2)}) async-start(), calls=%async_computation.8 | async-start | bytes 2949120 | tf_op jit(solution)/shard_map/all_gather | solution.py:354
  25.1 24.8 %collective-permute-start.3 = (bf16[1,512,1024]{2,1,0:T(8,128)(2,1)}, bf16[1,512,1024]{2,1,0:T(8,128)(2,1)S(1)}, u32[]{:S(2)}, u32[]{:S(2)}) collective-permute-start(bf16[1,512,1024]{2,1,0:T(8,128)(2,1)} %param.18), channel_id=1, source_target_pairs={{0,1},{1,0},{2,3},{3,2},{4,5},{5,4},{6,7},{7,6},{8,9},{9,8},{10,11... | collective-permute-start | bytes 3145736 | tf_op jit(solution)/shard_map/ppermute | solution.py:278
  26.3 24.0 %collective-permute-start.4 = (bf16[1,512,1024]{2,1,0:T(8,128)(2,1)}, bf16[1,512,1024]{2,1,0:T(8,128)(2,1)S(1)}, u32[]{:S(2)}, u32[]{:S(2)}) collective-permute-start(bf16[1,512,1024]{2,1,0:T(8,128)(2,1)} %param.18), channel_id=1, source_target_pairs={{0,2},{1,3},{2,0},{3,1},{4,6},{5,7},{6,4},{7,5},{8,10},{9,11},{10,... | collective-permute-start | bytes 3145736 | tf_op jit(solution)/shard_map/ppermute | solution.py:278
  27.2 1.5 collective-permute-start.7
  31.0 177.8 %reduce-scatter.4.cloned.1.call-start = ((), (), s32[]{:S(2)}) async-start(), calls=%async_computation.3 | async-start | bytes 589824 | tf_op jit(solution)/shard_map/reduce_scatter | solution.py:357
  54.0 21.1 %collective-permute-start.5 = (bf16[1,256,1024]{2,1,0:T(8,128)(2,1)}, bf16[1,256,1024]{2,1,0:T(8,128)(2,1)S(1)}, u32[]{:S(2)}, u32[]{:S(2)}) collective-permute-start(bf16[1,256,1024]{2,1,0:T(8,128)(2,1)} %get-tuple-element.57), channel_id=1, source_target_pairs={{0,2},{1,3},{2,0},{3,1},{4,6},{5,7},{6,4},{7,5},{8,10},{9,11},{10,... | collective-permute-start | bytes 1572872 | tf_op jit(solution)/shard_map/ppermute | solution.py:278
  55.4 19.7 %collective-permute-start.6 = (bf16[1,256,1024]{2,1,0:T(8,128)(2,1)}, bf16[1,256,1024]{2,1,0:T(8,128)(2,1)S(1)}, u32[]{:S(2)}, u32[]{:S(2)}) collective-permute-start(bf16[1,256,1024]{2,1,0:T(8,128)(2,1)} %get-tuple-element.58), channel_id=1, source_target_pairs={{0,1},{1,0},{2,3},{3,2},{4,5},{5,4},{6,7},{7,6},{8,9},{9,8},{10,11... | collective-permute-start | bytes 1572872 | tf_op jit(solution)/shard_map/ppermute | solution.py:278
  72.8 27.3 %collective-permute-start.9 = (bf16[1,512,1024]{2,1,0:T(8,128)(2,1)}, bf16[1,512,1024]{2,1,0:T(8,128)(2,1)S(1)}, u32[]{:S(2)}, u32[]{:S(2)}) collective-permute-start(bf16[1,512,1024]{2,1,0:T(8,128)(2,1)} %after.1), channel_id=1, source_target_pairs={{0,2},{1,3},{2,0},{3,1},{4,6},{5,7},{6,4},{7,5},{8,10},{9,11},{10,... | collective-permute-start | bytes 3145736 | tf_op jit(solution)/shard_map/ppermute | solution.py:278
  74.5 25.6 %collective-permute-start.8 = (bf16[1,512,1024]{2,1,0:T(8,128)(2,1)}, bf16[1,512,1024]{2,1,0:T(8,128)(2,1)S(1)}, u32[]{:S(2)}, u32[]{:S(2)}) collective-permute-start(bf16[1,512,1024]{2,1,0:T(8,128)(2,1)} %after.1), channel_id=1, source_target_pairs={{0,1},{1,0},{2,3},{3,2},{4,5},{5,4},{6,7},{7,6},{8,9},{9,8},{10,11... | collective-permute-start | bytes 3145736 | tf_op jit(solution)/shard_map/ppermute | solution.py:278
  103.6 15.5 %collective-permute-start.10 = (bf16[1,256,1024]{2,1,0:T(8,128)(2,1)}, bf16[1,256,1024]{2,1,0:T(8,128)(2,1)S(1)}, u32[]{:S(2)}, u32[]{:S(2)}) collective-permute-start(bf16[1,256,1024]{2,1,0:T(8,128)(2,1)} %get-tuple-element.69), channel_id=1, source_target_pairs={{0,2},{1,3},{2,0},{3,1},{4,6},{5,7},{6,4},{7,5},{8,10},{9,11},{10,... | collective-permute-start | bytes 1572872 | tf_op jit(solution)/shard_map/ppermute | solution.py:278
  104.1 15.0 %collective-permute-start.11 = (bf16[1,256,1024]{2,1,0:T(8,128)(2,1)}, bf16[1,256,1024]{2,1,0:T(8,128)(2,1)S(1)}, u32[]{:S(2)}, u32[]{:S(2)}) collective-permute-start(bf16[1,256,1024]{2,1,0:T(8,128)(2,1)} %get-tuple-element.70), channel_id=1, source_target_pairs={{0,1},{1,0},{2,3},{3,2},{4,5},{5,4},{6,7},{7,6},{8,9},{9,8},{10,11... | collective-permute-start | bytes 1572872 | tf_op jit(solution)/shard_map/ppermute | solution.py:278
  120.1 22.7 %copy-start.7 = (bf16[4,1,512,256]{3,2,1,0:T(8,128)(2,1)S(1)}, bf16[4,1,512,256]{3,2,1,0:T(8,128)(2,1)}, u32[]{:S(2)}) copy-start(bf16[4,1,512,256]{3,2,1,0:T(8,128)(2,1)} %get-tuple-element.64) | copy-start | bytes 3145732
  147.1 82.4 %reduce-scatter.6.cloned.1.call-start = ((), (), s32[]{:S(2)}) async-start(), calls=%async_computation.4 | async-start | bytes 4718592 | tf_op jit(solution)/shard_map/reduce_scatter | solution.py:357
  162.5 121.8 %reduce-scatter.8.cloned.1.call-start = ((), (), s32[]{:S(2)}) async-start(), calls=%async_computation.5 | async-start | bytes 1769472 | tf_op jit(solution)/shard_map/reduce_scatter | solution.py:357
  164.2 58.6 %collective-permute-start.12 = (bf16[512,1024]{1,0:T(8,128)(2,1)}, bf16[512,1024]{1,0:T(8,128)(2,1)S(1)}, u32[]{:S(2)}, u32[]{:S(2)}) collective-permute-start(bf16[512,1024]{1,0:T(8,128)(2,1)} %get-tuple-element.72), channel_id=1, source_target_pairs={{0,1},{1,0},{2,3},{3,2},{4,5},{5,4},{6,7},{7,6},{8,9},{9,8},{10,11... | collective-permute-start | bytes 3145736 | tf_op jit(solution)/shard_map/ppermute | solution.py:278
  165.6 59.1 %collective-permute-start.13 = (bf16[512,1024]{1,0:T(8,128)(2,1)}, bf16[512,1024]{1,0:T(8,128)(2,1)S(1)}, u32[]{:S(2)}, u32[]{:S(2)}) collective-permute-start(bf16[512,1024]{1,0:T(8,128)(2,1)} %get-tuple-element.73), channel_id=1, source_target_pairs={{0,2},{1,3},{2,0},{3,1},{4,6},{5,7},{6,4},{7,5},{8,10},{9,11},{10,... | collective-permute-start | bytes 3145736 | tf_op jit(solution)/shard_map/ppermute | solution.py:278
  167.1 57.6 %collective-permute-start.14 = (bf16[512,1024]{1,0:T(8,128)(2,1)}, bf16[512,1024]{1,0:T(8,128)(2,1)S(1)}, u32[]{:S(2)}, u32[]{:S(2)}) collective-permute-start(bf16[512,1024]{1,0:T(8,128)(2,1)} %get-tuple-element.74), channel_id=1, source_target_pairs={{0,3},{1,2},{2,1},{3,0},{4,7},{5,6},{6,5},{7,4},{8,11},{9,10},{10,... | collective-permute-start | bytes 3145736 | tf_op jit(solution)/shard_map/ppermute | solution.py:278
  167.7 33.5 %copy-start.1 = (bf16[2048,1024]{1,0:T(8,128)(2,1)S(1)}, bf16[2048,1024]{1,0:T(8,128)(2,1)}, u32[]{:S(2)}) copy-start(bf16[2048,1024]{1,0:T(8,128)(2,1)} %get-tuple-element.82) | copy-start | bytes 12582916
  201.2 6.8 %copy-start.2 = (bf16[4,1,512,768]{3,2,1,0:T(8,128)(2,1)S(1)}, bf16[4,1,512,768]{3,2,1,0:T(8,128)(2,1)}, u32[]{:S(2)}) copy-start(bf16[4,1,512,768]{3,2,1,0:T(8,128)(2,1)} %attend_back.1) | copy-start | bytes 9437188
  208.8 18.1 %collective-permute-start.32 = (bf16[32,1024]{1,0:T(8,128)(2,1)}, bf16[32,1024]{1,0:T(8,128)(2,1)S(1)}, u32[]{:S(2)}, u32[]{:S(2)}) collective-permute-start(bf16[32,1024]{1,0:T(8,128)(2,1)} %bitcast.148), channel_id=1, source_target_pairs={{0,0},{4,1},{8,2},{12,3},{16,4},{20,5},{24,6},{28,7},{1,8},{5,9},{... | collective-permute-start | bytes 196616 | tf_op jit(solution)/shard_map/ppermute | solution.py:286
  216.9 7.8 %copy-start.10 = (bf16[1,512,1024]{2,1,0:T(8,128)(2,1)S(1)}, bf16[1,512,1024]{2,1,0:T(8,128)(2,1)}, u32[]{:S(2)}) copy-start(bf16[1,512,1024]{2,1,0:T(8,128)(2,1)} %param.18) | copy-start | bytes 3145732
  216.9 7.8 %copy-start.11 = (bf16[512,1024]{1,0:T(8,128)(2,1)S(1)}, bf16[512,1024]{1,0:T(8,128)(2,1)}, u32[]{:S(2)}) copy-start(bf16[512,1024]{1,0:T(8,128)(2,1)} %get-tuple-element.71) | copy-start | bytes 3145732
  219.3 33.9 %collective-permute-start.17 = (bf16[1,256,1024]{2,1,0:T(8,128)(2,1)}, bf16[1,256,1024]{2,1,0:T(8,128)(2,1)}, u32[]{:S(2)}, u32[]{:S(2)}) collective-permute-start(bf16[1,256,1024]{2,1,0:T(8,128)(2,1)} %get-tuple-element.103), channel_id=1, source_target_pairs={{0,1},{1,0},{2,3},{3,2},{4,5},{5,4},{6,7},{7,6},{8,9},{9,8},{10,11... | collective-permute-start | bytes 1572872 | tf_op jit(solution)/shard_map/ppermute | solution.py:278
  222.8 27.5 %collective-permute-start.15 = (bf16[1,256,1024]{2,1,0:T(8,128)(2,1)}, bf16[1,256,1024]{2,1,0:T(8,128)(2,1)}, u32[]{:S(2)}, u32[]{:S(2)}) collective-permute-start(bf16[1,256,1024]{2,1,0:T(8,128)(2,1)} %get-tuple-element.104), channel_id=1, source_target_pairs={{0,2},{1,3},{2,0},{3,1},{4,6},{5,7},{6,4},{7,5},{8,10},{9,11},{10,... | collective-permute-start | bytes 1572872 | tf_op jit(solution)/shard_map/ppermute | solution.py:278
  238.6 6.7 %copy-start.24 = (f32[4,1024]{1,0:T(4,128)S(1)}, f32[4,1024]{1,0:T(4,128)}, u32[]{:S(2)}) copy-start(f32[4,1024]{1,0:T(4,128)} %get-tuple-element.86) | copy-start | bytes 49156
  238.6 7.4 %copy-start.4 = (bf16[1024,1024]{1,0:T(8,128)(2,1)S(1)}, bf16[1024,1024]{1,0:T(8,128)(2,1)}, u32[]{:S(2)}) copy-start(bf16[1024,1024]{1,0:T(8,128)(2,1)} %get-tuple-element.83.refs_0_) | copy-start | bytes 6291460
  246.7 8.0 %collective-permute-start.19 = (f32[8,384]{1,0:T(8,128)S(1)}, f32[8,384]{1,0:T(8,128)S(1)}, u32[]{:S(2)}, u32[]{:S(2)}) collective-permute-start(f32[8,384]{1,0:T(8,128)S(1)} %get-tuple-element.115), channel_id=1, source_target_pairs={{0,1},{1,0},{2,3},{3,2},{4,5},{5,4},{6,7},{7,6},{8,9},{9,8},{10,11... | collective-permute-start | bytes 36872 | tf_op jit(solution)/shard_map/ppermute | solution.py:278
  248.2 6.5 %collective-permute-start.21 = (f32[8,384]{1,0:T(8,128)S(1)}, f32[8,384]{1,0:T(8,128)S(1)}, u32[]{:S(2)}, u32[]{:S(2)}) collective-permute-start(f32[8,384]{1,0:T(8,128)S(1)} %get-tuple-element.116), channel_id=1, source_target_pairs={{0,3},{1,2},{2,1},{3,0},{4,7},{5,6},{6,5},{7,4},{8,11},{9,10},{10,... | collective-permute-start | bytes 36872 | tf_op jit(solution)/shard_map/ppermute | solution.py:278
  249.7 5.0 %collective-permute-start.20 = (f32[8,384]{1,0:T(8,128)S(1)}, f32[8,384]{1,0:T(8,128)S(1)}, u32[]{:S(2)}, u32[]{:S(2)}) collective-permute-start(f32[8,384]{1,0:T(8,128)S(1)} %get-tuple-element.117), channel_id=1, source_target_pairs={{0,2},{1,3},{2,0},{3,1},{4,6},{5,7},{6,4},{7,5},{8,10},{9,11},{10,... | collective-permute-start | bytes 36872 | tf_op jit(solution)/shard_map/ppermute | solution.py:278
  251.6 37.7 %collective-permute-start.16 = (bf16[1,512,1024]{2,1,0:T(8,128)(2,1)S(1)}, bf16[1,512,1024]{2,1,0:T(8,128)(2,1)}, u32[]{:S(2)}, u32[]{:S(2)}) collective-permute-start(bf16[1,512,1024]{2,1,0:T(8,128)(2,1)S(1)} %pad_maximum_fusion), channel_id=1, source_target_pairs={{0,1},{1,0},{2,3},{3,2},{4,5},{5,4},{6,7},{7,6},{8,9},{9,8},{10,11... | collective-permute-start | bytes 3145736 | tf_op jit(solution)/shard_map/ppermute | solution.py:278
  254.5 34.9 %collective-permute-start.18 = (bf16[1,512,1024]{2,1,0:T(8,128)(2,1)S(1)}, bf16[1,512,1024]{2,1,0:T(8,128)(2,1)}, u32[]{:S(2)}, u32[]{:S(2)}) collective-permute-start(bf16[1,512,1024]{2,1,0:T(8,128)(2,1)S(1)} %pad_maximum_fusion.1), channel_id=1, source_target_pairs={{0,2},{1,3},{2,0},{3,1},{4,6},{5,7},{6,4},{7,5},{8,10},{9,11},{10,... | collective-permute-start | bytes 3145736 | tf_op jit(solution)/shard_map/ppermute | solution.py:278
  254.8 1.2 collective-permute-start.22
  256.0 6.6 %collective-permute-start.23 = (f32[384]{0:T(512)S(1)}, f32[384]{0:T(512)S(1)}, u32[]{:S(2)}, u32[]{:S(2)}) collective-permute-start(f32[384]{0:T(512)S(1)} %get-tuple-element.97), channel_id=1, source_target_pairs={{0,8},{4,12},{8,16},{12,20},{16,24},{20,28},{24,0},{28,4},{1,9},{5... | collective-permute-start | bytes 4616 | tf_op jit(solution)/shard_map/ppermute | solution.py:334
  256.6 6.8 %collective-permute-start.25 = (f32[384]{0:T(512)S(1)}, f32[384]{0:T(512)S(1)}, u32[]{:S(2)}, u32[]{:S(2)}) collective-permute-start(f32[384]{0:T(512)S(1)} %get-tuple-element.98), channel_id=1, source_target_pairs={{0,24},{4,28},{8,0},{12,4},{16,8},{20,12},{24,16},{28,20},{1,25},{... | collective-permute-start | bytes 4616 | tf_op jit(solution)/shard_map/ppermute | solution.py:334
  261.1 4.6 %collective-permute-start.24 = (f32[384]{0:T(512)S(1)}, f32[384]{0:T(512)S(1)}, u32[]{:S(2)}, u32[]{:S(2)}) collective-permute-start(f32[384]{0:T(512)S(1)} %get-tuple-element.99), channel_id=1, source_target_pairs={{0,16},{4,20},{8,24},{12,28},{16,0},{20,4},{24,8},{28,12},{1,17},{... | collective-permute-start | bytes 4616 | tf_op jit(solution)/shard_map/ppermute | solution.py:334
  262.6 17.0 %collective-permute-start.28 = (bf16[32,1024]{1,0:T(8,128)(2,1)S(1)}, bf16[32,1024]{1,0:T(8,128)(2,1)S(1)}, u32[]{:S(2)}, u32[]{:S(2)}) collective-permute-start(bf16[32,1024]{1,0:T(8,128)(2,1)S(1)} %get-tuple-element.107), channel_id=1, source_target_pairs={{0,3},{1,2},{2,1},{3,0},{4,7},{5,6},{6,5},{7,4},{8,11},{9,10},{10,... | collective-permute-start | bytes 196616 | tf_op jit(solution)/shard_map/ppermute | solution.py:278
  263.4 18.5 %collective-permute-start.27 = (bf16[32,1024]{1,0:T(8,128)(2,1)S(1)}, bf16[32,1024]{1,0:T(8,128)(2,1)S(1)}, u32[]{:S(2)}, u32[]{:S(2)}) collective-permute-start(bf16[32,1024]{1,0:T(8,128)(2,1)S(1)} %get-tuple-element.108), channel_id=1, source_target_pairs={{0,2},{1,3},{2,0},{3,1},{4,6},{5,7},{6,4},{7,5},{8,10},{9,11},{10,... | collective-permute-start | bytes 196616 | tf_op jit(solution)/shard_map/ppermute | solution.py:278
  265.7 16.3 %collective-permute-start.26 = (bf16[32,1024]{1,0:T(8,128)(2,1)S(1)}, bf16[32,1024]{1,0:T(8,128)(2,1)S(1)}, u32[]{:S(2)}, u32[]{:S(2)}) collective-permute-start(bf16[32,1024]{1,0:T(8,128)(2,1)S(1)} %get-tuple-element.109), channel_id=1, source_target_pairs={{0,1},{1,0},{2,3},{3,2},{4,5},{5,4},{6,7},{7,6},{8,9},{9,8},{10,11... | collective-permute-start | bytes 196616 | tf_op jit(solution)/shard_map/ppermute | solution.py:278
  266.4 23.0 %copy-start.26 = (f32[384]{0:T(512)}, f32[384]{0:T(512)S(1)}, u32[]{:S(2)}) copy-start(f32[384]{0:T(512)S(1)} %add_add_fusion.1.refs_1_) | copy-start | bytes 4612
  267.0 29.7 %copy-start.28 = (f32[32]{0:T(128)}, f32[32]{0:T(128)S(1)}, u32[]{:S(2)}) copy-start(f32[32]{0:T(128)S(1)} %get-tuple-element.151) | copy-start | bytes 388
  285.9 8.5 %collective-permute-start.31 = (bf16[32,768]{1,0:T(8,128)(2,1)S(1)}, bf16[32,768]{1,0:T(8,128)(2,1)S(1)}, u32[]{:S(2)}, u32[]{:S(2)}) collective-permute-start(bf16[32,768]{1,0:T(8,128)(2,1)S(1)} %get-tuple-element.111), channel_id=1, source_target_pairs={{0,3},{1,2},{2,1},{3,0},{4,7},{5,6},{6,5},{7,4},{8,11},{9,10},{10,... | collective-permute-start | bytes 147464 | tf_op jit(solution)/shard_map/ppermute | solution.py:278
  287.3 7.1 %collective-permute-start.30 = (bf16[32,768]{1,0:T(8,128)(2,1)S(1)}, bf16[32,768]{1,0:T(8,128)(2,1)S(1)}, u32[]{:S(2)}, u32[]{:S(2)}) collective-permute-start(bf16[32,768]{1,0:T(8,128)(2,1)S(1)} %get-tuple-element.112), channel_id=1, source_target_pairs={{0,2},{1,3},{2,0},{3,1},{4,6},{5,7},{6,4},{7,5},{8,10},{9,11},{10,... | collective-permute-start | bytes 147464 | tf_op jit(solution)/shard_map/ppermute | solution.py:278
  289.0 5.4 %collective-permute-start.29 = (bf16[32,768]{1,0:T(8,128)(2,1)S(1)}, bf16[32,768]{1,0:T(8,128)(2,1)S(1)}, u32[]{:S(2)}, u32[]{:S(2)}) collective-permute-start(bf16[32,768]{1,0:T(8,128)(2,1)S(1)} %get-tuple-element.113), channel_id=1, source_target_pairs={{0,1},{1,0},{2,3},{3,2},{4,5},{5,4},{6,7},{7,6},{8,9},{9,8},{10,11... | collective-permute-start | bytes 147464 | tf_op jit(solution)/shard_map/ppermute | solution.py:278
  (22 other events, 31.4 us)
Sparse Core Ops, SparseCore 0:
  24.4 29.3 all-gather.6
  55.3 28.0 all-gather.8
  85.7 33.3 all-gather.10
  147.2 30.3 reduce-scatter.3
  179.8 49.6 reduce-scatter.5
  231.8 35.3 reduce-scatter.7
where the time goes:
time: 310 us; the launch traced here: 304 us
  Pallas kernels  160 us (52%)
  waiting for transfers between devices  47.1 us (15%)
  starting transfers between devices  43.2 us (14%)
  local copies, waits for them, and re-layouts  18.7 us (6%)
  between operations  14.9 us (5%)
  matrix products  11 us (4%)
  other arithmetic  9.12 us (3%)
    ppermute x27, waiting for transfers between devices, seq_swap(): return lax.ppermute(array, 'seq', [(i, i ^ k) for i in range(self.seq)])  41.1 us
    ppermute x27, starting transfers between devices, seq_swap(): return lax.ppermute(array, 'seq', [(i, i ^ k) for i in range(self.seq)])  34.3 us
    pallas_call x1, Pallas kernels, attend_back(): pl.pallas_call(functools.partial(attend_back_kernel, pair, head_dim), gri...  33.5 us
    pallas_call x1, Pallas kernels, turnabout(): pl.pallas_call(functools.partial(turnabout_kernel, stacked, len(pieces),...  22.7 us
    pallas_call x3, Pallas kernels, unproject(): pl.pallas_call(unproject_kernel, grid=(rows // block,), in_specs=[pl.Bloc...  22.2 us
    pallas_call x1, Pallas kernels, attend(): pl.pallas_call(functools.partial(attend_kernel, pair, head_dim), grid_spe...  18.6 us
    pallas_call x2, Pallas kernels, project(): pl.pallas_call(functools.partial(project_kernel, head_dim, lanes, shard,...  15.9 us
    pallas_call x1, Pallas kernels, outer(): pl.pallas_call(functools.partial(outer_kernel, count), grid=(count, halve...  15.4 us
  transfers between devices with their start and end apart: 39, of which 11 were waited for; matrix products, arithmetic and copies ran while one was open for 8% of the time, Pallas kernels for 43%

commit v1 on v0

--- a/solution.py
+++ b/solution.py
@@ -314,10 +314,6 @@
             return near
         first, second = cut(near[1], near[2], wait)
         return near + [self.seq_swap(first, 2), self.seq_swap(second, 1)]
-
-    def seq_reduce_far(self, part):
-        half = part.shape[1] // 2
-        return self.seq_swap(part[:, half:], 2), self.seq_swap(part[:, :half], 1)
 
     def seq_reduce_near(self, parts, far):
         half = parts[0].shape[1] // 2
@@ -812,18 +808,41 @@
                         out[:, target + r * stride : target + r * stride + size] = piece
 
 
-def hand(place, pieces, moves):
+def hand(place, pieces, moves, columns):
     count = len(pieces)
-    rows, columns = pieces[0].shape
+    rows = pieces[0].shape[0]
     vmem = pl.BlockSpec(memory_space=pltpu.VMEM)
     return pl.pallas_call(
         functools.partial(hand_kernel, count, moves),
         in_specs=[pl.BlockSpec(memory_space=pltpu.SMEM)] + [vmem] * count,
         out_specs=vmem,
-        out_shape=jax.ShapeDtypeStruct((rows, count * columns), full),
+        out_shape=jax.ShapeDtypeStruct((rows, columns), full),
         compiler_params=pltpu.CompilerParams(vmem_limit_bytes=kernel_memory),
         name="hand",
     )(place, *pieces)
+
+
+def settle_kernel(count, *refs):
+    total = refs[count][...]
+    for ref in refs[:count]:
+        total = total + ref[...].astype(full)
+    refs[-1][...] = total.astype(low)
+
+
+def settle(parts, bias, wait):
+    rows, width = parts[0].shape
+    block = rows // 4 if rows % 64 == 0 else rows
+    spec = pl.BlockSpec((block, width), lambda i: (i, 0))
+    return pl.pallas_call(
+        functools.partial(settle_kernel, len(parts)),
+        grid=(rows // block,),
+        in_specs=[spec] * len(parts) + [pl.BlockSpec((1, width), lambda i: (0, 0))] + [anywhere] * len(wait),
+        out_specs=spec,
+        out_shape=jax.ShapeDtypeStruct((rows, width), low),
+        compiler_params=pltpu.CompilerParams(vmem_limit_bytes=kernel_memory),
+        cost_estimate=effort(3 * rows / 512),
+        name="settle",
+    )(*parts, bias, *wait)
 
 
 def finish_kernel(x_ref, cot_ref, own_ref, first_ref, second_ref, *refs):
@@ -850,14 +869,17 @@
     )(x, cot, own, first, second, *wait)
 
 
-def unproject_kernel(x_ref, mixed_ref, hidden_ref, in_ref, up_ref, norms_ref, *refs):
-    out_ref, sums_ref = refs[-2:]
+def unproject_kernel(outs, x_ref, mixed_ref, hidden_ref, in_ref, up_ref, norms_ref, *refs):
+    out_refs, sums_ref = refs[-1 - outs : -1], refs[-1]
     unit, _ = normalised(x_ref[...].astype(full))
     width, columns = x_ref.shape[1], mixed_ref.shape[1]
     in_weight = in_ref[:, : width // in_ref.shape[0], :columns].reshape(width, columns)
     attn = contract(mixed_ref[...], in_weight, 1, 1)
     ff = contract(hidden_ref[...], up_ref[...], 1, 1)
-    out_ref[...] = (attn * norms_ref[0:1, :] + ff * norms_ref[2:3, :]).astype(low)
+    result = (attn * norms_ref[0:1, :] + ff * norms_ref[2:3, :]).astype(low)
+    part = result.shape[0] // outs
+    for k, out_ref in enumerate(out_refs):
+        out_ref[...] = result[k * part : (k + 1) * part]
     sums = [attn * unit, attn, ff * unit, ff]
     sums = jnp.concatenate([jnp.sum(a, axis=0, keepdims=True) for a in sums], 0)
 
@@ -870,13 +892,13 @@
         sums_ref[...] += sums
 
 
-def unproject(x, mixed, hidden, in_weight, up_weight, norms, block, first, count, wait):
+def unproject(x, mixed, hidden, in_weight, up_weight, norms, block, first, count, wait, outs=1):
     rows, width = count * block, x.shape[1]
     whole = lambda i: (0, 0)
     step = lambda i: (i + first, 0)
     here = lambda i: (i, 0)
     return pl.pallas_call(
-        unproject_kernel,
+        functools.partial(unproject_kernel, outs),
         grid=(rows // block,),
         in_specs=[
             pl.BlockSpec((block, width), step),
@@ -887,23 +909,15 @@
             pl.BlockSpec((4, width), whole),
         ]
         + [anywhere] * len(wait),
-        out_specs=[pl.BlockSpec((block, width), here), pl.BlockSpec((4, width), whole)],
-        out_shape=[
-            jax.ShapeDtypeStruct((rows, width), low),
+        out_specs=[pl.BlockSpec((block // outs, width), here)] * outs + [pl.BlockSpec((4, width), whole)],
+        out_shape=[jax.ShapeDtypeStruct((rows // outs, width), low)] * outs
+        + [
             jax.ShapeDtypeStruct((4, width), full),
         ],
         compiler_params=pltpu.CompilerParams(vmem_limit_bytes=kernel_memory),
         cost_estimate=effort(18 * rows / 2048),
         name="unproject",
     )(x, mixed, hidden, in_weight, up_weight, norms, *wait)
-
-
-def reduce_steps(at, far, near):
-    if at.seq != 4:
-        got = [at.seq_swap(a, k + 1) for k, a in enumerate(near())]
-        return [], got + [at.seq_swap(far, at.seq - 1)]
-    first = at.seq_reduce_far(far)
-    return first, list(at.seq_reduce_near(near(), first))
 
 
 def on_device(
@@ -1011,22 +1025,29 @@
     mixed_grad = mixed_grad.reshape(rows, 3 * span)
     in_grad = lax.optimization_barrier(contract(normed_attn, mixed_grad, 0, 0).astype(low))
     in_grad = in_grad.reshape(dp, seq * shard, 3 * span)
-    wait = (out_grads,)
+    wait = (out_grads, *out_near)
     last = (seq - 1) * seqs
     weights = (head_all, up_all, norms)
-    far_grad, far_sums = unproject(x, mixed_grad, hidden_grad, *weights, block, last, seqs, wait)
+    halves = 2 if seq == 4 and seqs == 1 else 1
+    *far_grad, far_sums = unproject(x, mixed_grad, hidden_grad, *weights, block, last, seqs, wait, halves)
     in_ready = after_big(in_grad, unit_sum_grads)
     in_grads = at.dp_reduce(in_ready)
-    near_grad, near_sums = unproject(x, mixed_grad, hidden_grad, *weights, block, seqs, last - seqs, (far_grad, in_ready))
+    near_grad, near_sums = unproject(x, mixed_grad, hidden_grad, *weights, block, seqs, last - seqs, (far_grad[0], in_ready))
     own_grad, own_sums = unproject(x, mixed_grad, hidden_grad, *weights, block, 0, seqs, (near_grad,))
     norm_sums = far_sums + near_sums + own_sums
     near_grad = near_grad.reshape(seq - 2, seqs, block, width)
-    _, unit_near = reduce_steps(
-        at, far_grad.reshape(seqs, block, width), lambda: [near_grad[k] for k in range(seq - 2)]
-    )
-    out_sum = out_part[0].astype(full) + sum(a.astype(full) for a in out_near)
-    output = tokens.astype(full) + out_sum.reshape(tokens.shape) + (bias_out + bias_down)
-    output = output.astype(low)
+    others = [near_grad[k] for k in range(seq - 2)]
+    if halves == 2:
+        first, second = (a.reshape(seqs, block // 2, width) for a in far_grad)
+        far = (at.seq_swap(second, 2), at.seq_swap(first, 1))
+        unit_near = list(at.seq_reduce_near(others, far))
+    else:
+        others = others + [far_grad[0].reshape(seqs, block, width)]
+        unit_near = [at.seq_swap(a, k + 1) for k, a in enumerate(others)]
+    bias = (bias_out + bias_down).reshape(1, width)
+    parts = [a.reshape(-1, width) for a in (tokens, out_part[0], *out_near)]
+    output = settle(parts, bias, (own_grad,)).reshape(tokens.shape)
+
     in_bias_sum = jnp.sum(mixed_grad.astype(full), axis=0).reshape(groups, 3, lanes)
     in_bias_sum = jnp.swapaxes(in_bias_sum, 0, 1).reshape(3, 1, span)
     in_bias_sum = lax.dynamic_update_slice_in_dim(jnp.zeros((3, seq, span), full), in_bias_sum, rank, 1)
@@ -1050,21 +1071,23 @@
 
     down_final = unit_sum_grads[:units].astype(full)
     up_final = unit_sum_grads[units:].reshape(seq, shard, dp * units)
+    out_final = at.from_heads(out_grads).astype(full)
+    own = dp * units
+    handed = jnp.concatenate([up_final, in_grads.reshape(seq, shard, 3 * span)], 2)
+    pieces = at.seq_exchange(lambda spot: pick(handed, spot, 0))
     up_moves = [(d * units, d * seq * units, units, units) for d in range(dp)]
-    up_final = hand(place, at.seq_exchange(lambda spot: pick(up_final, spot, 0)), up_moves)
-    out_final = at.from_heads(out_grads).astype(full)
-    in_split = in_grads.reshape(seq, shard, 3 * span)
     in_moves = [
-        ((g * 3 + kind) * lanes, kind * width + g * lanes, span, lanes) for g in range(groups) for kind in range(3)
+        (own + (g * 3 + kind) * lanes, kind * width + g * lanes, span, lanes) for g in range(groups) for kind in range(3)
     ]
-    in_final = hand(place, at.seq_exchange(lambda spot: pick(in_split, spot, 0)), in_moves)
+    up_final = hand(place, pieces, up_moves, dp * seq * units)
+    in_final = hand(place, pieces, in_moves, 3 * width)
     total = at.small_reduce(small)
     flat = [a.reshape(-1, width) for a in (tokens, cotangent, own_grad)]
     if len(unit_near) == 2:
         others = [a.reshape(-1, width) for a in unit_near]
     else:
         others = [sum(a.astype(full) for a in unit_near).reshape(-1, width), jnp.zeros_like(flat[0])]
-    token_grad = finish(*flat, *others, (output, total, up_final)).reshape(seqs, block, width)
+    token_grad = finish(*flat, *others, (output, pieces[0])).reshape(seqs, block, width)
     (query_key_bias, value_bias, out_bias, up_bias_grad, *norm_grads) = [
         total[edges[i] : edges[i + 1]] for i in range(8)
     ]

time: 310 us -> 302 us (0.974)
  waiting for transfers between devices: 47.1 us -> 42 us
  Pallas kernels: 160 us -> 165 us
  local copies, waits for them, and re-layouts: 18.7 us -> 15.3 us
    ppermute x27 -> x24, waiting for transfers between devices: 41.1 us -> 33.4 us  [seq_swap(): return lax.ppermute(array, 'seq', [(i, i ^ k) for i in range(self.seq)])]
    pallas_call x3 -> x4, Pallas kernels: 22.2 us -> 26.7 us  [the longest x3 22.2 us: unproject(): pl.pallas_call(functools.partial(unproject_kernel, outs), grid=(rows // b...]
    ppermute x27 -> x24, starting transfers between devices: 34.3 us -> 30.9 us  [seq_swap(): return lax.ppermute(array, 'seq', [(i, i ^ k) for i in range(self.seq)])]
    unnamed x65 -> x53, local copies, waits for them, and re-layouts: 8.97 us -> 9.05 us
  transfers between devices with their start and end apart: 39 -> 36, of which waited for: 11 -> 13; matrix products, arithmetic and copies ran while one was open for 8% -> 7% of each run, Pallas kernels for 43% -> 45%
where the time goes in v1:
time: 302 us; the launch traced here: 297 us
  Pallas kernels  165 us (55%)
  waiting for transfers between devices  42 us (14%)
  starting transfers between devices  40.2 us (13%)
  local copies, waits for them, and re-layouts  15.3 us (5%)
  between operations  14.8 us (5%)
  matrix products  11.2 us (4%)
  other arithmetic  8.39 us (3%)
    ppermute x24, waiting for transfers between devices, seq_swap(): return lax.ppermute(array, 'seq', [(i, i ^ k) for i in range(self.seq)])  33.4 us
    pallas_call x1, Pallas kernels, attend_back(): pl.pallas_call(functools.partial(attend_back_kernel, pair, head_dim), gri...  33.4 us
    ppermute x24, starting transfers between devices, seq_swap(): return lax.ppermute(array, 'seq', [(i, i ^ k) for i in range(self.seq)])  30.9 us
    pallas_call x1, Pallas kernels, turnabout(): pl.pallas_call(functools.partial(turnabout_kernel, stacked, len(pieces),...  22.7 us
    pallas_call x3, Pallas kernels, unproject(): pl.pallas_call(functools.partial(unproject_kernel, outs), grid=(rows // b...  22.2 us
    pallas_call x1, Pallas kernels, attend(): pl.pallas_call(functools.partial(attend_kernel, pair, head_dim), grid_spe...  18.6 us
    pallas_call x2, Pallas kernels, project(): pl.pallas_call(functools.partial(project_kernel, head_dim, lanes, shard,...  15.9 us
    pallas_call x1, Pallas kernels, outer(): pl.pallas_call(functools.partial(outer_kernel, count), grid=(count, halve...  15.4 us
  transfers between devices with their start and end apart: 36, of which 13 were waited for; matrix products, arithmetic and copies ran while one was open for 7% of the time, Pallas kernels for 45%

profile of v1, /device:TPU:0, one launch (start us, length us, event | category | flops | bytes accessed | tf_op | source)
XLA Modules:
  0.0 296.8 jit_solution(5040119235790742348)
XLA Ops:
  7.2 2.0 deal.1
  9.2 2.9 collective-permute-start
  12.1 1.5 collective-permute-start.1
  13.7 3.7 %collective-permute-done.refs_1_ = bf16[80,1024]{1,0:T(8,128)(2,1)S(1)} collective-permute-done((bf16[80,1024]{1,0:T(8,128)(2,1)}, bf16[80,1024]{1,0:T(8,128)(2,1)S(1)}, u32[]{:S(2)}, u32[]{:S(2)}) %collective-permute-start) | collective-permute-done | bytes 163872 | tf_op jit(solution)/shard_map/ppermute | solution.py:278
  17.4 4.1 %collective-permute-done.1.refs_2_ = bf16[80,1024]{1,0:T(8,128)(2,1)S(1)} collective-permute-done((bf16[80,1024]{1,0:T(8,128)(2,1)}, bf16[80,1024]{1,0:T(8,128)(2,1)S(1)}, u32[]{:S(2)}, u32[]{:S(2)}) %collective-permute-start.1) | collective-permute-done | bytes 163872 | tf_op jit(solution)/shard_map/ppermute | solution.py:278
  22.2 2.0 gather_heads.1
  27.2 1.5 collective-permute-start.7
  29.3 1.7 join.1
  31.1 18.8 %collective-permute-done.3.x_ref = bf16[1,512,1024]{2,1,0:T(8,128)(2,1)S(1)} collective-permute-done((bf16[1,512,1024]{2,1,0:T(8,128)(2,1)}, bf16[1,512,1024]{2,1,0:T(8,128)(2,1)S(1)}, u32[]{:S(2)}, u32[]{:S(2)}) %collective-permute-start.3) | collective-permute-done | bytes 1048608 | tf_op jit(solution)/shard_map/ppermute | solution.py:278
  51.8 2.2 cut.2
  54.0 1.4 collective-permute-start.5
  55.4 1.6 collective-permute-start.6
  60.5 10.5 %project.2 = (bf16[2048,1024]{1,0:T(8,128)(2,1)}, bf16[2048,1024]{1,0:T(8,128)(2,1)}, bf16[2048,1024]{1,0:T(8,128)(2,1)}, bf16[2048,768]{1,0:T(8,128)(2,1)}) custom-call(s32[1]{0:T(128)} %bitcast.1.place, bf16[8,160,768]{2,1,0:T(8,128)(2,1)} %bitcast.98, f32[1,768]{1,0:T(1,128)} %reshape.243.bias_ref, f32[4,1024]{1,0:T(4,128)} %maximum_convert_fusion.norms_ref, ...), custom_call_target="tpu_custom_call" | custom-call | flops 9900000256 | bytes 1 | tf_op jit(solution)/shard_map/project/pallas_call | solution.py:439
  71.0 2.3 after.1
  73.5 1.5 collective-permute-start.9
  76.7 5.4 %project.3 = (bf16[2048,1024]{1,0:T(8,128)(2,1)}, bf16[2048,1024]{1,0:T(8,128)(2,1)}, bf16[2048,1024]{1,0:T(8,128)(2,1)}, bf16[2048,768]{1,0:T(8,128)(2,1)}) custom-call(s32[1]{0:T(128)} %bitcast.1.place, bf16[8,160,768]{2,1,0:T(8,128)(2,1)} %bitcast.99, ...), custom_call_target="tpu_custom_call", output_to_operand_aliasing={{0}: (8, {}), {1}: (9, {}), {2}: (10, {}), {3}: (11, {})} | custom-call | flops 3300000000 | bytes 1 | tf_op jit(solution)/shard_map/project/pallas_call | solution.py:439
  82.1 18.6 %attend.1 = (f32[4,1,512,256]{3,2,1,0:T(8,128)}, bf16[4,1,512,256]{3,2,1,0:T(8,128)(2,1)}, f32[4,1,2,2,512]{4,3,2,1,0:T(2,128)}) custom-call(s32[1]{0:T(128)} %bitcast.1.place, bf16[4,1,512,768]{3,2,1,0:T(8,128)(2,1)} %bitcast.95), custom_call_target="tpu_custom_call" | custom-call | flops 19800000512 | bytes 1 | tf_op jit(solution)/shard_map/attend/pallas_call | solution.py:529
  102.0 2.2 cut.3
  104.7 1.7 collective-permute-start.11
  106.5 11.3 %expand.1 = (bf16[2048,1024]{1,0:T(8,128)(2,1)}, bf16[2048,1024]{1,0:T(8,128)(2,1)}) custom-call(bf16[2048,1024]{1,0:T(8,128)(2,1)} %get-tuple-element.66.x_ref.refs_2_, bf16[1024,1024]{1,0:T(8,128)(2,1)} %all-gather.9.cloned.1.call-done.weight_ref.up_ref, f32[1,1024]{1,0:T(1,128)} %fusion.13.bias_ref, bf16[2048,256]{1,0:T(8,128)(2,1)} %bitcast.110), custom_call_target="tpu_custom_call" | custom-call | flops 13200000000 | bytes 1 | tf_op jit(solution)/shard_map/expand/pallas_call | solution.py:650
  117.7 1.4 all-gather.11.cloned.1.call-done
  120.5 22.7 %turnabout.1 = (bf16[512,1024]{1,0:T(8,128)(2,1)}, bf16[512,1024]{1,0:T(8,128)(2,1)}, bf16[512,1024]{1,0:T(8,128)(2,1)}, bf16[512,1024]{1,0:T(8,128)(2,1)}, bf16...) custom-call(bf16[2048,256]{1,0:T(8,128)(2,1)} %bitcast.111, ...), custom_call_target="tpu_custom_call" | custom-call | flops 15399999488 | bytes 1 | tf_op jit(solution)/shard_map/turnabout/pallas_call | solution.py:731
  143.2 4.3 %convolution_convert_fusion.1.refs_1_ = bf16[256,1024]{1,0:T(8,128)(2,1)} fusion(bf16[2048,256]{1,0:T(8,128)(2,1)S(1)} %bitcast.112, bf16[2048,1024]{1,0:T(8,128)(2,1)} %get-tuple-element.80.refs_1_), kind=kOutput, calls=%fused_computation.3 | convolution fusion | flops 1074003968 | bytes 5767168 | tf_op jit(solution)/shard_map/dot_general | solution.py:475
  147.5 15.4 %outer.1.refs_0_ = bf16[8,256,1024]{2,1,0:T(8,128)(2,1)} custom-call(bf16[2048,1024]{1,0:T(8,128)(2,1)} %get-tuple-element.68.active_ref.refs_0_, bf16[2048,1024]{1,0:T(8,128)(2,1)} %get-tuple-element.80.refs_1_, bf16[2048,1024]{1,0:T(8,128)(2,1)} %get-tuple-element.66.x_ref.refs_2_, bf16[2048,1024]{1,0:T(8,128)(2,1)} %get-tuple-element.81.refs_3_.hidden_ref), custom_call_target="tpu_custom_call" | custom-call | flops 11000000512 | bytes 1 | tf_op jit(solution)/shard_map/outer/pallas_call | solution.py:783
  166.1 1.5 collective-permute-start.13
  168.5 33.4 %attend_back.1 = bf16[4,1,512,768]{3,2,1,0:T(8,128)(2,1)} custom-call(s32[1]{0:T(128)} %bitcast.1.place, bf16[4,1,512,768]{3,2,1,0:T(8,128)(2,1)} %bitcast.96, f32[4,1,512,256]{3,2,1,0:T(8,128)} %get-tuple-element.77.exact_ref, bf16[4,1,512,256]{3,2,1,0:T(8,128)(2,1)} %bitcast.142, f32[4,1,2,2,512]{4,3,2,1,0:T(2,128)} %get-tuple-element.79.lse_ref, ...), custom_call_target="tpu_custom_call" | custom-call | flops 36300001280 | bytes 1 | tf_op jit(solution)/shard_map/attend_back/pallas_call | solution.py:609
  201.9 2.6 convert_reduce_fusion
  204.8 6.9 %convolution_convert_fusion = bf16[1024,768]{1,0:T(8,128)(2,1)} fusion(bf16[2048,1024]{1,0:T(8,128)(2,1)} %get-tuple-element.83, bf16[2048,768]{1,0:T(8,128)(2,1)S(1)} %bitcast.94), kind=kOutput, calls=%fused_computation.2 | convolution fusion | flops 3222011904 | bytes 8912896 | tf_op jit(solution)/shard_map/dot_general | solution.py:475
  211.9 1.5 collective-permute-start.29
  213.9 6.5 %unproject.3 = (bf16[256,1024]{1,0:T(8,128)(2,1)}, bf16[256,1024]{1,0:T(8,128)(2,1)}, f32[4,1024]{1,0:T(4,128)}) custom-call(bf16[2048,1024]{1,0:T(8,128)(2,1)} %get-tuple-element.76.x_ref, bf16[2048,768]{1,0:T(8,128)(2,1)} %bitcast.91, bf16[2048,1024]{1,0:T(8,128)(2,1)} %get-tuple-element.81.refs_3_.hidden_ref, bf16[8,160,768]{2,1,0:T(8,128)(2,1)} %bitcast.100, ...), custom_call_target="tpu_custom_call" | custom-call | flops 4950000128 | bytes 1 | tf_op jit(solution)/shard_map/unproject/pallas_call | solution.py:900
  220.4 3.1 %collective-permute-start.17 = (bf16[1,256,1024]{2,1,0:T(8,128)(2,1)}, bf16[1,256,1024]{2,1,0:T(8,128)(2,1)S(1)}, u32[]{:S(2)}, u32[]{:S(2)}) collective-permute-start(bf16[1,256,1024]{2,1,0:T(8,128)(2,1)} %bitcast.139), channel_id=1, source_target_pairs={{0,1},{1,0},{2,3},{3,2},{4,5},{5,4},{6,7},{7,6},{8,9},{9,8},{10,11... | collective-permute-start | bytes 1572872 | tf_op jit(solution)/shard_map/ppermute | solution.py:278
  223.5 1.9 collective-permute-start.15
  226.1 3.8 %reduce-scatter.6.cloned.1.call-done = bf16[1,256,1024]{2,1,0:T(8,128)(2,1)} async-done(((bf16[8,256,1024]{2,1,0:T(8,128)(2,1)}), bf16[1,256,1024]{2,1,0:T(8,128)(2,1)}) %reduce-scatter.6.cloned.1.call-update) | async-done | bytes 524304 | tf_op jit(solution)/shard_map/reduce_scatter | solution.py:353
  230.0 9.0 %unproject.4 = (bf16[1024,1024]{1,0:T(8,128)(2,1)}, f32[4,1024]{1,0:T(4,128)}) custom-call(bf16[2048,1024]{1,0:T(8,128)(2,1)} %get-tuple-element.76.x_ref, bf16[2048,768]{1,0:T(8,128)(2,1)} %bitcast.92, bf16[2048,1024]{1,0:T(8,128)(2,1)} %get-tuple-element.81.refs_3_.hidden_ref, bf16[8,160,768]{2,1,0:T(8,128)(2,1)} %bitcast.101, ...), custom_call_target="tpu_custom_call" | custom-call | flops 9900000256 | bytes 1 | tf_op jit(solution)/shard_map/unproject/pallas_call | solution.py:900
  239.0 6.6 %unproject.5 = (bf16[512,1024]{1,0:T(8,128)(2,1)}, f32[4,1024]{1,0:T(4,128)}) custom-call(bf16[2048,1024]{1,0:T(8,128)(2,1)} %get-tuple-element.76.x_ref, bf16[2048,768]{1,0:T(8,128)(2,1)} %bitcast.93, bf16[2048,1024]{1,0:T(8,128)(2,1)} %get-tuple-element.81.refs_3_.hidden_ref, bf16[8,160,768]{2,1,0:T(8,128)(2,1)} %bitcast.102, ...), custom_call_target="tpu_custom_call" | custom-call | flops 4950000128 | bytes 1 | tf_op jit(solution)/shard_map/unproject/pallas_call | solution.py:900
  247.1 1.6 collective-permute-start.22
  248.7 1.9 collective-permute-start.24
  251.0 1.5 collective-permute-start.18
  253.5 4.5 %settle.1 = bf16[512,1024]{1,0:T(8,128)(2,1)} custom-call(bf16[512,1024]{1,0:T(8,128)(2,1)} %bitcast.136, bf16[512,1024]{1,0:T(8,128)(2,1)} %get-tuple-element.72.refs_1_, bf16[512,1024]{1,0:T(8,128)(2,1)} %collective-permute-done.12.refs_1_.refs_2_, bf16[512,1024]{1,0:T(8,128)(2,1)} %collective-permute-done.13.refs_2_.refs_3_, ...), custom_call_target="tpu_custom_call" | custom-call | flops 3300000000 | bytes 1 | tf_op jit(solution)/shard_map/settle/pallas_call | solution.py:836
  258.7 5.2 %collective-permute-start.27 = (f32[384]{0:T(512)S(1)}, f32[384]{0:T(512)S(1)}, u32[]{:S(2)}, u32[]{:S(2)}) collective-permute-start(f32[384]{0:T(512)S(1)} %get-tuple-element.101), channel_id=1, source_target_pairs={{0,16},{4,20},{8,24},{12,28},{16,0},{20,4},{24,8},{28,12},{1,17},{... | collective-permute-start | bytes 4616 | tf_op jit(solution)/shard_map/ppermute | solution.py:330
  265.4 2.0 collective-permute-done.28
  269.1 1.5 fusion.2
  271.9 2.3 collective-permute-start.21
  274.1 3.1 %collective-permute-done.18 = bf16[1,512,1024]{2,1,0:T(8,128)(2,1)} collective-permute-done((bf16[1,512,1024]{2,1,0:T(8,128)(2,1)S(1)}, bf16[1,512,1024]{2,1,0:T(8,128)(2,1)}, u32[]{:S(2)}, u32[]{:S(2)}) %collective-permute-start.18) | collective-permute-done | bytes 1048608 | tf_op jit(solution)/shard_map/ppermute | solution.py:278
  277.2 1.9 collective-permute-done.16
  279.1 5.0 %finish.1 = bf16[512,1024]{1,0:T(8,128)(2,1)} custom-call(bf16[512,1024]{1,0:T(8,128)(2,1)} %bitcast.137, bf16[512,1024]{1,0:T(8,128)(2,1)} %bitcast.104, bf16[512,1024]{1,0:T(8,128)(2,1)} %get-tuple-element.85.refs_6_.own_ref, bf16[512,1024]{1,0:T(8,128)(2,1)} %bitcast.37.first_ref, bf16[512,1024]{1,0:T(8,128)(2,1)} %bitcast.40.second_ref, ...), custom_call_target="tpu_custom_call" | custom-call | flops 3300000000 | bytes 1 | tf_op jit(solution)/shard_map/finish/pallas_call | solution.py:860
  285.4 1.9 hand.3
  287.4 1.8 hand.2
  (168 shorter events, 30.1 us)
Async XLA Ops:
  7.2 49.8 %all-gather.7.cloned.1.call-start = ((), (), s32[]{:S(2)}) async-start(), calls=%async_computation.6 | async-start | bytes 2211840 | tf_op jit(solution)/shard_map/all_gather | solution.py:350
  9.2 8.2 %collective-permute-start = (bf16[80,1024]{1,0:T(8,128)(2,1)}, bf16[80,1024]{1,0:T(8,128)(2,1)S(1)}, u32[]{:S(2)}, u32[]{:S(2)}) collective-permute-start(bf16[80,1024]{1,0:T(8,128)(2,1)} %get-tuple-element.54), channel_id=1, source_target_pairs={{0,1},{1,0},{2,3},{3,2},{4,5},{5,4},{6,7},{7,6},{8,9},{9,8},{10,11... | collective-permute-start | bytes 491528 | tf_op jit(solution)/shard_map/ppermute | solution.py:278
  12.1 9.4 %collective-permute-start.1 = (bf16[80,1024]{1,0:T(8,128)(2,1)}, bf16[80,1024]{1,0:T(8,128)(2,1)S(1)}, u32[]{:S(2)}, u32[]{:S(2)}) collective-permute-start(bf16[80,1024]{1,0:T(8,128)(2,1)} %get-tuple-element.55), channel_id=1, source_target_pairs={{0,2},{1,3},{2,0},{3,1},{4,6},{5,7},{6,4},{7,5},{8,10},{9,11},{10,... | collective-permute-start | bytes 491528 | tf_op jit(solution)/shard_map/ppermute | solution.py:278
  13.7 7.9 %collective-permute-start.2 = (bf16[80,1024]{1,0:T(8,128)(2,1)}, bf16[80,1024]{1,0:T(8,128)(2,1)S(1)}, u32[]{:S(2)}, u32[]{:S(2)}) collective-permute-start(bf16[80,1024]{1,0:T(8,128)(2,1)} %get-tuple-element.56), channel_id=1, source_target_pairs={{0,3},{1,2},{2,1},{3,0},{4,7},{5,6},{6,5},{7,4},{8,11},{9,10},{10,... | collective-permute-start | bytes 491528 | tf_op jit(solution)/shard_map/ppermute | solution.py:278
  17.4 4.2 %copy-start.14 = (bf16[80,1024]{1,0:T(8,128)(2,1)}, bf16[80,1024]{1,0:T(8,128)(2,1)S(1)}, u32[]{:S(2)}) copy-start(bf16[80,1024]{1,0:T(8,128)(2,1)S(1)} %collective-permute-done.refs_1_) | copy-start | bytes 491524
  24.3 82.2 %all-gather.9.cloned.1.call-start = ((), (), s32[]{:S(2)}) async-start(), calls=%async_computation.7 | async-start | bytes 2359296 | tf_op jit(solution)/shard_map/all_gather | solution.py:350
  25.0 94.1 %all-gather.11.cloned.1.call-start = ((), (), s32[]{:S(2)}) async-start(), calls=%async_computation.8 | async-start | bytes 2949120 | tf_op jit(solution)/shard_map/all_gather | solution.py:350
  25.1 24.8 %collective-permute-start.3 = (bf16[1,512,1024]{2,1,0:T(8,128)(2,1)}, bf16[1,512,1024]{2,1,0:T(8,128)(2,1)S(1)}, u32[]{:S(2)}, u32[]{:S(2)}) collective-permute-start(bf16[1,512,1024]{2,1,0:T(8,128)(2,1)} %param.18), channel_id=1, source_target_pairs={{0,1},{1,0},{2,3},{3,2},{4,5},{5,4},{6,7},{7,6},{8,9},{9,8},{10,11... | collective-permute-start | bytes 3145736 | tf_op jit(solution)/shard_map/ppermute | solution.py:278
  26.3 24.0 %collective-permute-start.4 = (bf16[1,512,1024]{2,1,0:T(8,128)(2,1)}, bf16[1,512,1024]{2,1,0:T(8,128)(2,1)S(1)}, u32[]{:S(2)}, u32[]{:S(2)}) collective-permute-start(bf16[1,512,1024]{2,1,0:T(8,128)(2,1)} %param.18), channel_id=1, source_target_pairs={{0,2},{1,3},{2,0},{3,1},{4,6},{5,7},{6,4},{7,5},{8,10},{9,11},{10,... | collective-permute-start | bytes 3145736 | tf_op jit(solution)/shard_map/ppermute | solution.py:278
  27.2 1.5 collective-permute-start.7
  31.0 180.9 %reduce-scatter.4.cloned.1.call-start = ((), (), s32[]{:S(2)}) async-start(), calls=%async_computation.3 | async-start | bytes 589824 | tf_op jit(solution)/shard_map/reduce_scatter | solution.py:353
  54.0 21.7 %collective-permute-start.5 = (bf16[1,256,1024]{2,1,0:T(8,128)(2,1)}, bf16[1,256,1024]{2,1,0:T(8,128)(2,1)S(1)}, u32[]{:S(2)}, u32[]{:S(2)}) collective-permute-start(bf16[1,256,1024]{2,1,0:T(8,128)(2,1)} %get-tuple-element.58), channel_id=1, source_target_pairs={{0,2},{1,3},{2,0},{3,1},{4,6},{5,7},{6,4},{7,5},{8,10},{9,11},{10,... | collective-permute-start | bytes 1572872 | tf_op jit(solution)/shard_map/ppermute | solution.py:278
  55.4 20.3 %collective-permute-start.6 = (bf16[1,256,1024]{2,1,0:T(8,128)(2,1)}, bf16[1,256,1024]{2,1,0:T(8,128)(2,1)S(1)}, u32[]{:S(2)}, u32[]{:S(2)}) collective-permute-start(bf16[1,256,1024]{2,1,0:T(8,128)(2,1)} %get-tuple-element.59), channel_id=1, source_target_pairs={{0,1},{1,0},{2,3},{3,2},{4,5},{5,4},{6,7},{7,6},{8,9},{9,8},{10,11... | collective-permute-start | bytes 1572872 | tf_op jit(solution)/shard_map/ppermute | solution.py:278
  73.3 27.4 %collective-permute-start.8 = (bf16[1,512,1024]{2,1,0:T(8,128)(2,1)}, bf16[1,512,1024]{2,1,0:T(8,128)(2,1)S(1)}, u32[]{:S(2)}, u32[]{:S(2)}) collective-permute-start(bf16[1,512,1024]{2,1,0:T(8,128)(2,1)} %after.1), channel_id=1, source_target_pairs={{0,1},{1,0},{2,3},{3,2},{4,5},{5,4},{6,7},{7,6},{8,9},{9,8},{10,11... | collective-permute-start | bytes 3145736 | tf_op jit(solution)/shard_map/ppermute | solution.py:278
  73.5 27.1 %collective-permute-start.9 = (bf16[1,512,1024]{2,1,0:T(8,128)(2,1)}, bf16[1,512,1024]{2,1,0:T(8,128)(2,1)S(1)}, u32[]{:S(2)}, u32[]{:S(2)}) collective-permute-start(bf16[1,512,1024]{2,1,0:T(8,128)(2,1)} %after.1), channel_id=1, source_target_pairs={{0,2},{1,3},{2,0},{3,1},{4,6},{5,7},{6,4},{7,5},{8,10},{9,11},{10,... | collective-permute-start | bytes 3145736 | tf_op jit(solution)/shard_map/ppermute | solution.py:278
  100.7 1.3 copy-start.5
  104.2 14.9 %collective-permute-start.10 = (bf16[1,256,1024]{2,1,0:T(8,128)(2,1)}, bf16[1,256,1024]{2,1,0:T(8,128)(2,1)S(1)}, u32[]{:S(2)}, u32[]{:S(2)}) collective-permute-start(bf16[1,256,1024]{2,1,0:T(8,128)(2,1)} %get-tuple-element.70), channel_id=1, source_target_pairs={{0,2},{1,3},{2,0},{3,1},{4,6},{5,7},{6,4},{7,5},{8,10},{9,11},{10,... | collective-permute-start | bytes 1572872 | tf_op jit(solution)/shard_map/ppermute | solution.py:278
  104.7 15.0 %collective-permute-start.11 = (bf16[1,256,1024]{2,1,0:T(8,128)(2,1)}, bf16[1,256,1024]{2,1,0:T(8,128)(2,1)S(1)}, u32[]{:S(2)}, u32[]{:S(2)}) collective-permute-start(bf16[1,256,1024]{2,1,0:T(8,128)(2,1)} %get-tuple-element.71), channel_id=1, source_target_pairs={{0,1},{1,0},{2,3},{3,2},{4,5},{5,4},{6,7},{7,6},{8,9},{9,8},{10,11... | collective-permute-start | bytes 1572872 | tf_op jit(solution)/shard_map/ppermute | solution.py:278
  120.5 22.7 %copy-start.6 = (bf16[4,1,512,256]{3,2,1,0:T(8,128)(2,1)S(1)}, bf16[4,1,512,256]{3,2,1,0:T(8,128)(2,1)}, u32[]{:S(2)}) copy-start(bf16[4,1,512,256]{3,2,1,0:T(8,128)(2,1)} %get-tuple-element.65) | copy-start | bytes 3145732
  147.4 82.5 %reduce-scatter.6.cloned.1.call-start = ((), (), s32[]{:S(2)}) async-start(), calls=%async_computation.4 | async-start | bytes 4718592 | tf_op jit(solution)/shard_map/reduce_scatter | solution.py:353
  162.9 1.2 copy-start.1
  162.9 1.5 copy-start.18
  162.9 106.2 %reduce-scatter.8.cloned.1.call-start = ((), (), s32[]{:S(2)}) async-start(), calls=%async_computation.5 | async-start | bytes 1769472 | tf_op jit(solution)/shard_map/reduce_scatter | solution.py:353
  165.1 48.4 %collective-permute-start.12 = (bf16[512,1024]{1,0:T(8,128)(2,1)}, bf16[512,1024]{1,0:T(8,128)(2,1)}, u32[]{:S(2)}, u32[]{:S(2)}) collective-permute-start(bf16[512,1024]{1,0:T(8,128)(2,1)} %get-tuple-element.73), channel_id=1, source_target_pairs={{0,1},{1,0},{2,3},{3,2},{4,5},{5,4},{6,7},{7,6},{8,9},{9,8},{10,11... | collective-permute-start | bytes 3145736 | tf_op jit(solution)/shard_map/ppermute | solution.py:278
  166.1 47.3 %collective-permute-start.13 = (bf16[512,1024]{1,0:T(8,128)(2,1)}, bf16[512,1024]{1,0:T(8,128)(2,1)}, u32[]{:S(2)}, u32[]{:S(2)}) collective-permute-start(bf16[512,1024]{1,0:T(8,128)(2,1)} %get-tuple-element.74), channel_id=1, source_target_pairs={{0,2},{1,3},{2,0},{3,1},{4,6},{5,7},{6,4},{7,5},{8,10},{9,11},{10,... | collective-permute-start | bytes 3145736 | tf_op jit(solution)/shard_map/ppermute | solution.py:278
  167.6 46.3 %collective-permute-start.14 = (bf16[512,1024]{1,0:T(8,128)(2,1)}, bf16[512,1024]{1,0:T(8,128)(2,1)}, u32[]{:S(2)}, u32[]{:S(2)}) collective-permute-start(bf16[512,1024]{1,0:T(8,128)(2,1)} %get-tuple-element.75), channel_id=1, source_target_pairs={{0,3},{1,2},{2,1},{3,0},{4,7},{5,6},{6,5},{7,4},{8,11},{9,10},{10,... | collective-permute-start | bytes 3145736 | tf_op jit(solution)/shard_map/ppermute | solution.py:278
  201.9 2.9 copy-start
  204.8 7.1 %copy-start.21 = (f32[1,1024]{1,0:T(1,128)S(1)}, f32[1,1024]{1,0:T(1,128)}, u32[]{:S(2)}) copy-start(f32[1,1024]{1,0:T(1,128)} %get-tuple-element.87) | copy-start | bytes 12292
  211.9 13.5 %collective-permute-start.29 = (bf16[32,1024]{1,0:T(8,128)(2,1)}, bf16[32,1024]{1,0:T(8,128)(2,1)S(1)}, u32[]{:S(2)}, u32[]{:S(2)}) collective-permute-start(bf16[32,1024]{1,0:T(8,128)(2,1)} %bitcast.120), channel_id=1, source_target_pairs={{0,0},{4,1},{8,2},{12,3},{16,4},{20,5},{24,6},{28,7},{1,8},{5,9},{... | collective-permute-start | bytes 196616 | tf_op jit(solution)/shard_map/ppermute | solution.py:286
  220.4 30.3 %collective-permute-start.17 = (bf16[1,256,1024]{2,1,0:T(8,128)(2,1)}, bf16[1,256,1024]{2,1,0:T(8,128)(2,1)S(1)}, u32[]{:S(2)}, u32[]{:S(2)}) collective-permute-start(bf16[1,256,1024]{2,1,0:T(8,128)(2,1)} %bitcast.139), channel_id=1, source_target_pairs={{0,1},{1,0},{2,3},{3,2},{4,5},{5,4},{6,7},{7,6},{8,9},{9,8},{10,11... | collective-permute-start | bytes 1572872 | tf_op jit(solution)/shard_map/ppermute | solution.py:278
  223.5 29.1 %collective-permute-start.15 = (bf16[1,256,1024]{2,1,0:T(8,128)(2,1)}, bf16[1,256,1024]{2,1,0:T(8,128)(2,1)S(1)}, u32[]{:S(2)}, u32[]{:S(2)}) collective-permute-start(bf16[1,256,1024]{2,1,0:T(8,128)(2,1)} %bitcast.138), channel_id=1, source_target_pairs={{0,2},{1,3},{2,0},{3,1},{4,6},{5,7},{6,4},{7,5},{8,10},{9,11},{10,... | collective-permute-start | bytes 1572872 | tf_op jit(solution)/shard_map/ppermute | solution.py:278
  239.0 6.7 %copy-start.19 = (f32[4,1024]{1,0:T(4,128)S(1)}, f32[4,1024]{1,0:T(4,128)}, u32[]{:S(2)}) copy-start(f32[4,1024]{1,0:T(4,128)} %get-tuple-element.88) | copy-start | bytes 49156
  239.0 6.7 %copy-start.20 = (f32[4,1024]{1,0:T(4,128)S(1)}, f32[4,1024]{1,0:T(4,128)}, u32[]{:S(2)}) copy-start(f32[4,1024]{1,0:T(4,128)} %get-tuple-element.89) | copy-start | bytes 49156
  239.0 7.4 %copy-start.3 = (bf16[1024,1024]{1,0:T(8,128)(2,1)S(1)}, bf16[1024,1024]{1,0:T(8,128)(2,1)}, u32[]{:S(2)}) copy-start(bf16[1024,1024]{1,0:T(8,128)(2,1)} %get-tuple-element.84.refs_0_) | copy-start | bytes 6291460
  247.1 5.9 %collective-permute-start.22 = (f32[8,384]{1,0:T(8,128)S(1)}, f32[8,384]{1,0:T(8,128)S(1)}, u32[]{:S(2)}, u32[]{:S(2)}) collective-permute-start(f32[8,384]{1,0:T(8,128)S(1)} %get-tuple-element.113), channel_id=1, source_target_pairs={{0,1},{1,0},{2,3},{3,2},{4,5},{5,4},{6,7},{7,6},{8,9},{9,8},{10,11... | collective-permute-start | bytes 36872 | tf_op jit(solution)/shard_map/ppermute | solution.py:278
  248.7 4.3 %collective-permute-start.23 = (f32[8,384]{1,0:T(8,128)S(1)}, f32[8,384]{1,0:T(8,128)S(1)}, u32[]{:S(2)}, u32[]{:S(2)}) collective-permute-start(f32[8,384]{1,0:T(8,128)S(1)} %get-tuple-element.115), channel_id=1, source_target_pairs={{0,2},{1,3},{2,0},{3,1},{4,6},{5,7},{6,4},{7,5},{8,10},{9,11},{10,... | collective-permute-start | bytes 36872 | tf_op jit(solution)/shard_map/ppermute | solution.py:278
  248.7 4.6 %collective-permute-start.24 = (f32[8,384]{1,0:T(8,128)S(1)}, f32[8,384]{1,0:T(8,128)S(1)}, u32[]{:S(2)}, u32[]{:S(2)}) collective-permute-start(f32[8,384]{1,0:T(8,128)S(1)} %get-tuple-element.114), channel_id=1, source_target_pairs={{0,3},{1,2},{2,1},{3,0},{4,7},{5,6},{6,5},{7,4},{8,11},{9,10},{10,... | collective-permute-start | bytes 36872 | tf_op jit(solution)/shard_map/ppermute | solution.py:278
  251.0 26.2 %collective-permute-start.18 = (bf16[1,512,1024]{2,1,0:T(8,128)(2,1)S(1)}, bf16[1,512,1024]{2,1,0:T(8,128)(2,1)}, u32[]{:S(2)}, u32[]{:S(2)}) collective-permute-start(bf16[1,512,1024]{2,1,0:T(8,128)(2,1)S(1)} %pad_maximum_fusion.1), channel_id=1, source_target_pairs={{0,2},{1,3},{2,0},{3,1},{4,6},{5,7},{6,4},{7,5},{8,10},{9,11},{10,... | collective-permute-start | bytes 3145736 | tf_op jit(solution)/shard_map/ppermute | solution.py:278
  252.9 26.3 %collective-permute-start.16 = (bf16[1,512,1024]{2,1,0:T(8,128)(2,1)S(1)}, bf16[1,512,1024]{2,1,0:T(8,128)(2,1)}, u32[]{:S(2)}, u32[]{:S(2)}) collective-permute-start(bf16[1,512,1024]{2,1,0:T(8,128)(2,1)S(1)} %pad_maximum_fusion), channel_id=1, source_target_pairs={{0,1},{1,0},{2,3},{3,2},{4,5},{5,4},{6,7},{7,6},{8,9},{9,8},{10,11... | collective-permute-start | bytes 3145736 | tf_op jit(solution)/shard_map/ppermute | solution.py:278
  253.4 4.6 %collective-permute-start.25 = (f32[4,384]{1,0:T(4,128)S(1)}, f32[4,384]{1,0:T(4,128)S(1)}, u32[]{:S(2)}, u32[]{:S(2)}) collective-permute-start(f32[4,384]{1,0:T(4,128)S(1)} %bitcast.124), channel_id=1, source_target_pairs={{0,4},{4,0},{8,12},{12,8},{16,20},{20,16},{24,28},{28,24},{1,5},{5... | collective-permute-start | bytes 18440 | tf_op jit(solution)/shard_map/ppermute | solution.py:341
  253.5 10.6 %copy-start.2 = (bf16[1,256,1024]{2,1,0:T(8,128)(2,1)S(1)}, bf16[1,256,1024]{2,1,0:T(8,128)(2,1)}, u32[]{:S(2)}) copy-start(bf16[1,256,1024]{2,1,0:T(8,128)(2,1)} %reduce-scatter.6.cloned.1.call-done) | copy-start | bytes 1572868
  258.1 6.8 %collective-permute-start.26 = (f32[384]{0:T(512)S(1)}, f32[384]{0:T(512)S(1)}, u32[]{:S(2)}, u32[]{:S(2)}) collective-permute-start(f32[384]{0:T(512)S(1)} %get-tuple-element.99), channel_id=1, source_target_pairs={{0,8},{4,12},{8,16},{12,20},{16,24},{20,28},{24,0},{28,4},{1,9},{5... | collective-permute-start | bytes 4616 | tf_op jit(solution)/shard_map/ppermute | solution.py:330
  258.7 6.8 %collective-permute-start.27 = (f32[384]{0:T(512)S(1)}, f32[384]{0:T(512)S(1)}, u32[]{:S(2)}, u32[]{:S(2)}) collective-permute-start(f32[384]{0:T(512)S(1)} %get-tuple-element.101), channel_id=1, source_target_pairs={{0,16},{4,20},{8,24},{12,28},{16,0},{20,4},{24,8},{28,12},{1,17},{... | collective-permute-start | bytes 4616 | tf_op jit(solution)/shard_map/ppermute | solution.py:330
  263.9 3.6 %collective-permute-start.28 = (f32[384]{0:T(512)S(1)}, f32[384]{0:T(512)S(1)}, u32[]{:S(2)}, u32[]{:S(2)}) collective-permute-start(f32[384]{0:T(512)S(1)} %get-tuple-element.100), channel_id=1, source_target_pairs={{0,24},{4,28},{8,0},{12,4},{16,8},{20,12},{24,16},{28,20},{1,25},{... | collective-permute-start | bytes 4616 | tf_op jit(solution)/shard_map/ppermute | solution.py:330
  269.1 20.1 %copy-start.22 = (f32[32]{0:T(128)}, f32[32]{0:T(128)S(1)}, u32[]{:S(2)}) copy-start(f32[32]{0:T(128)S(1)} %get-tuple-element.149) | copy-start | bytes 388
  270.6 13.4 %collective-permute-start.19 = (bf16[32,1792]{1,0:T(8,128)(2,1)S(1)}, bf16[32,1792]{1,0:T(8,128)(2,1)S(1)}, u32[]{:S(2)}, u32[]{:S(2)}) collective-permute-start(bf16[32,1792]{1,0:T(8,128)(2,1)S(1)} %get-tuple-element.109), channel_id=1, source_target_pairs={{0,1},{1,0},{2,3},{3,2},{4,5},{5,4},{6,7},{7,6},{8,9},{9,8},{10,11... | collective-permute-start | bytes 344072 | tf_op jit(solution)/shard_map/ppermute | solution.py:278
  270.8 13.3 %collective-permute-start.20 = (bf16[32,1792]{1,0:T(8,128)(2,1)S(1)}, bf16[32,1792]{1,0:T(8,128)(2,1)S(1)}, u32[]{:S(2)}, u32[]{:S(2)}) collective-permute-start(bf16[32,1792]{1,0:T(8,128)(2,1)S(1)} %get-tuple-element.110), channel_id=1, source_target_pairs={{0,2},{1,3},{2,0},{3,1},{4,6},{5,7},{6,4},{7,5},{8,10},{9,11},{10,... | collective-permute-start | bytes 344072 | tf_op jit(solution)/shard_map/ppermute | solution.py:278
  271.9 12.3 %collective-permute-start.21 = (bf16[32,1792]{1,0:T(8,128)(2,1)S(1)}, bf16[32,1792]{1,0:T(8,128)(2,1)S(1)}, u32[]{:S(2)}, u32[]{:S(2)}) collective-permute-start(bf16[32,1792]{1,0:T(8,128)(2,1)S(1)} %get-tuple-element.107), channel_id=1, source_target_pairs={{0,3},{1,2},{2,1},{3,0},{4,7},{5,6},{6,5},{7,4},{8,11},{9,10},{10,... | collective-permute-start | bytes 344072 | tf_op jit(solution)/shard_map/ppermute | solution.py:278
  (13 other events, 10.3 us)
Sparse Core Ops, SparseCore 0:
  24.4 29.3 all-gather.6
  55.4 28.0 all-gather.8
  85.7 33.3 all-gather.10
  147.6 30.3 reduce-scatter.3
  180.2 49.6 reduce-scatter.5
  232.2 35.1 reduce-scatter.7
